TPU v7x, 256 devices: a whole 4x4x8 slice. The times are simulated.
256 devices in a mesh: layer: 16 (over z, x_hi), latent: 16 (over x_lo, y, core).
Axes of the slice: x: 4 (x_hi: 2, x_lo: 2; x = x_hi * 2 + x_lo), y: 4, z: 8, core: 2. Of those that a mesh axis runs over, the one named last changes fastest.
Arguments:
- activations: bfloat16 [16, 1024, 2048], P('layer', 'latent'), may hold values from -6 to 6
- cotangents: bfloat16 [16, 1024, 2048], P('layer', 'latent'), may hold values from -0.375 to 0.375
- enc_weight: bfloat16 [16, 2048, 8192], P('layer', None, 'latent'), may hold values from -0.03125 to 0.03125
- dec_weight: bfloat16 [16, 8192, 2048], P('layer', 'latent'), may hold values from -0.03125 to 0.03125
- enc_bias: float32 [8192], P('latent'), may hold values from -3 to 3
- active_mask: int32 [1024, 8192], P(None, 'latent'), may hold values from 0 to 1, as said below
Outputs:
- enc_grad: bfloat16 [16, 2048, 8192], P('layer', None, 'latent')
- dec_grad: bfloat16 [16, 8192, 2048], P('layer', 'latent')
- bias_grad: float32 [8192], P('latent')
Inputs may be any that keep to these rules, and one draw needn't show every extreme that they name: `active_mask`: every token has exactly 64 ones among the 8192 latents.
All inputs are finite; a program needn't handle non-finite values.
Results may differ from a plain program's by a relative error of at most 0.007.
Values may be sent and summed in bfloat16 or wider, within the bound.
No kernel may reach another device: no remote copies, remote signals or barrier semaphores. Data moves between devices by JAX's collectives and lax.ppermute only.
A program may use at most 64 MiB of HBM per device.

v0:
```python
import jax
import jax.numpy as jnp
from jax import lax
from jax.sharding import PartitionSpec as P


def local(activations, cotangents, enc_weight, dec_weight, enc_bias, active_mask):
    whole_acts = lax.all_gather(activations[0], "latent", axis=0, tiled=True)
    whole_cots = lax.all_gather(cotangents[0], "latent", axis=0, tiled=True)
    enc_slab = enc_weight[0]
    dec_slab = dec_weight[0]
    mask_float = active_mask.astype(jnp.float32)
    pre_terms = jnp.dot(whole_acts, enc_slab, preferred_element_type=jnp.float32)
    cot_terms = lax.dot_general(
        whole_cots, dec_slab, (((1,), (1,)), ((), ())), preferred_element_type=jnp.float32
    )
    preact = lax.psum(pre_terms, "layer") + enc_bias[None, :]
    code = (mask_float * preact).astype(jnp.bfloat16)
    code_cot = lax.psum(cot_terms, "layer")
    pre_cot = (mask_float * code_cot).astype(jnp.bfloat16)
    dec_grad = lax.dot_general(
        code, whole_cots, (((0,), (0,)), ((), ())), preferred_element_type=jnp.float32
    )
    enc_grad = lax.dot_general(
        whole_acts, pre_cot, (((0,), (0,)), ((), ())), preferred_element_type=jnp.float32
    )
    bias_grad = jnp.sum(pre_cot.astype(jnp.float32), axis=0)
    return (enc_grad.astype(jnp.bfloat16)[None], dec_grad.astype(jnp.bfloat16)[None], bias_grad)


def solution(mesh):
    return jax.shard_map(
        local,
        mesh=mesh,
        in_specs=(
            P("layer", "latent", None),
            P("layer", "latent", None),
            P("layer", None, "latent"),
            P("layer", "latent", None),
            P("latent"),
            P(None, "latent"),
        ),
        out_specs=(P("layer", None, "latent"), P("layer", "latent", None), P("latent")),
        check_vma=False,
    )
```

profile of v0, /device:TPU:2, one launch (start us, length us, event | category | flops | bytes accessed | tf_op | source)
XLA Modules:
  0.0 334.7 jit_solution(9405549789907204633)
XLA Ops:
  7.2 0.0 copy-start
  7.2 0.0 all-gather.5.cloned.1.call-start
  7.2 0.7 all-gather.5.cloned.1.call-update
  7.9 0.0 all-gather.7.cloned.1.call-start
  8.0 0.7 all-gather.7.cloned.1.call-update
  8.7 0.0 all-reduce.3.cloned.1.call-start
  8.7 43.8 %all-gather.5.cloned.1.call-done = bf16[1,1024,2048]{2,1,0:T(8,128)(2,1)} async-done(((bf16[1,64,2048]{2,1,0:T(8,128)(2,1)}), bf16[1,1024,2048]{2,1,0:T(8,128)(2,1)}) %all-gather.5.cloned.1.call-update) | async-done | bytes 4194320 | tf_op jit(solution)/shard_map/all_gather | solution.py:9
  52.5 0.0 copy-done
  52.5 5.9 %fusion.6 = f32[1024,512]{1,0:T(8,128)} fusion(bf16[1,1024,2048]{2,1,0:T(8,128)(2,1)} %all-gather.5.cloned.1.call-done, bf16[1,512,2048]{2,1,0:T(8,128)(2,1)S(1)} %copy-done), kind=kOutput, calls=%fused_computation.6 | convolution fusion | flops 2147483648 | bytes 8388608 | tf_op jit(solution)/shard_map/dot_general | solution.py:14
  58.3 36.0 %all-gather.7.cloned.1.call-done = bf16[1,1024,2048]{2,1,0:T(8,128)(2,1)} async-done(((bf16[1,64,2048]{2,1,0:T(8,128)(2,1)}), bf16[1,1024,2048]{2,1,0:T(8,128)(2,1)}) %all-gather.7.cloned.1.call-update) | async-done | bytes 4194320 | tf_op jit(solution)/shard_map/all_gather | solution.py:8
  94.3 6.5 %fusion = f32[1024,512]{1,0:T(8,128)} fusion(bf16[1,1024,2048]{2,1,0:T(8,128)(2,1)} %all-gather.7.cloned.1.call-done, bf16[1,2048,512]{2,1,0:T(8,128)(2,1)} %param.8), kind=kOutput, calls=%fused_computation | convolution fusion | flops 2147483648 | bytes 8388608 | tf_op jit(solution)/shard_map/dot_general | solution.py:13
  100.8 0.0 all-reduce.3.cloned.1.call-update
  100.9 208.7 %all-reduce.3.cloned.1.call-done = (f32[1024,512]{1,0:T(8,128)}, f32[1024,512]{1,0:T(8,128)}) async-done(((f32[1024,512]{1,0:T(8,128)}, f32[1024,512]{1,0:T(8,128)}), (f32[1024,512]{1,0:T(8,128)}, f32[1024,512]{1,0:T(8,128)})) %all-reduce.3.cloned.1.call-update) | async-done | bytes 4194320 | tf_op jit(solution)/shard_map/psum | solution.py:19
  309.6 0.0 copy-start.1
  309.6 3.5 %convert_reduce_fusion = (f32[512]{0:T(512)}, bf16[1024,512]{1,0:T(8,128)(2,1)S(1)}) fusion(f32[1024,512]{1,0:T(8,128)} %get-tuple-element.6, s32[1024,512]{1,0:T(8,128)} %param.11), kind=kLoop, calls=%fused_computation.14 | loop fusion | flops 2620928 | bytes 5244928 | tf_op jit(solution)/shard_map/reduce_sum | solution.py:27
  313.1 0.0 copy-done.1
  313.1 3.8 %fusion.14 = bf16[1,2048,512]{1,2,0:T(8,128)(2,1)} fusion(bf16[1024,512]{1,0:T(8,128)(2,1)S(1)} %get-tuple-element.9, bf16[1,1024,2048]{2,1,0:T(8,128)(2,1)S(1)} %copy-done.1), kind=kOutput, calls=%fused_computation.10 | convolution fusion | flops 2148532224 | bytes 7340032 | tf_op jit(solution)/shard_map/dot_general | solution.py:24
  316.9 0.0 copy-start.2
  316.9 3.9 %copy.9 = bf16[1,2048,512]{2,1,0:T(8,128)(2,1)} copy(bf16[1,2048,512]{1,2,0:T(8,128)(2,1)} %fusion.14) | data formatting | bytes 4194304
  320.8 0.0 copy-done.2
  320.8 7.3 %fusion.17 = bf16[1,512,2048]{2,1,0:T(8,128)(2,1)} fusion(bf16[1,1024,2048]{2,1,0:T(8,128)(2,1)} %all-gather.5.cloned.1.call-done, f32[1024,512]{1,0:T(8,128)} %get-tuple-element.7, s32[1024,512]{1,0:T(8,128)} %param.11, f32[512]{0:T(512)S(1)} %copy-done.2), kind=kOutput, calls=%fused_computation.11 | convolution fusion | flops 2150629376 | bytes 10487808 | tf_op jit(solution)/shard_map/dot_general | solution.py:21
Async XLA Ops:
  7.2 45.3 %copy-start = (bf16[1,512,2048]{2,1,0:T(8,128)(2,1)S(1)}, bf16[1,512,2048]{2,1,0:T(8,128)(2,1)}, u32[]{:S(2)}) copy-start(bf16[1,512,2048]{2,1,0:T(8,128)(2,1)} %param.9) | copy-start | bytes 6291460
  7.2 45.3 %all-gather.5.cloned.1.call-start = ((), (), s32[]{:S(2)}) async-start(), calls=%async_computation | async-start | bytes 4456448 | tf_op jit(solution)/shard_map/all_gather | solution.py:9
  7.9 86.4 %all-gather.7.cloned.1.call-start = ((), (), s32[]{:S(2)}) async-start(), calls=%async_computation.1 | async-start | bytes 4456448 | tf_op jit(solution)/shard_map/all_gather | solution.py:8
  8.7 300.9 %all-reduce.3.cloned.1.call-start = ((), (), s32[]{:S(2)}) async-start(), calls=%async_computation.2 | async-start | bytes 8388608 | tf_op jit(solution)/shard_map/psum | solution.py:19
  309.6 3.5 %copy-start.1 = (bf16[1,1024,2048]{2,1,0:T(8,128)(2,1)S(1)}, bf16[1,1024,2048]{2,1,0:T(8,128)(2,1)}, u32[]{:S(2)}) copy-start(bf16[1,1024,2048]{2,1,0:T(8,128)(2,1)} %all-gather.7.cloned.1.call-done) | copy-start | bytes 12582916
  316.9 3.9 %copy-start.2 = (f32[512]{0:T(512)S(1)}, f32[512]{0:T(512)}, u32[]{:S(2)}) copy-start(f32[512]{0:T(512)} %param.10) | copy-start | bytes 6148
Sparse Core Ops, SparseCore 0:
  9.9 42.5 all-gather.4
  54.3 39.9 all-gather.6
  101.0 208.5 all-reduce.2
where the time goes:
time: 335 us
  waiting for transfers between devices  290 us (87%)
  matrix products  23.5 us (7%)
  between operations  13.8 us (4%)
  local copies, waits for them, and re-layouts  3.94 us (1%)
  other arithmetic  3.51 us (1%)
    psum x1, waiting for transfers between devices, local(): code_cot = lax.psum(cot_terms, 'layer')  209 us
    all_gather x1, waiting for transfers between devices, local(): whole_cots = lax.all_gather(cotangents[0], 'latent', axis=0, tiled=True)  43.8 us
    all_gather x1, waiting for transfers between devices, local(): whole_acts = lax.all_gather(activations[0], 'latent', axis=0, tiled=True)  36 us
    dot_general x1, matrix products, local(): lax.dot_general(code, whole_cots, (((0,), (0,)), ((), ())), preferred_ele...  7.34 us
  transfers between devices with their start and end apart: 3, of which 3 were waited for; matrix products, arithmetic and copies ran while one was open for 2% of the time, Pallas kernels for 0%

commit v1 on v0

v1 whole, which is shorter than its diff:
```python
import jax
import jax.numpy as jnp
from jax import lax
from jax.experimental import pallas as pl
from jax.experimental.pallas import tpu as pltpu
from jax.sharding import PartitionSpec as P

KEEP = 64
VMEM = 56 * 1024 * 1024


def take(values, lanes):
    return jnp.take_along_axis(values, lanes, axis=1, mode="promise_in_bounds")


def tiles_of(array):
    return [array[:, at : at + 128] for at in range(0, array.shape[1], 128)]


def rank_kernel(mask_ref, rank_ref, slot_ref):
    mask = mask_ref[...]
    rows, latents = mask.shape
    half = rows // 2
    shape = (latents, latents)
    upper = lax.broadcasted_iota(jnp.int32, shape, 0) <= lax.broadcasted_iota(jnp.int32, shape, 1)
    upper = upper.astype(jnp.float32).astype(jnp.bfloat16)
    ones = mask.astype(jnp.float32).astype(jnp.bfloat16)
    count = jnp.dot(ones, upper, preferred_element_type=jnp.float32).astype(jnp.int32)
    rank_ref[...] = jnp.where(mask > 0, count - 1, -1)
    tiles = tiles_of(count)
    lane = lax.broadcasted_iota(jnp.int32, (rows, 128), 1)
    place = lane % KEEP
    tile = jnp.zeros((rows, 128), jnp.int32)
    for part in tiles[:-1]:
        tile += jnp.where(take(part, jnp.full((rows, 128), 127, jnp.int32)) <= place, 1, 0)
    at = jnp.zeros((rows, 128), jnp.int32)
    for step in (64, 32, 16, 8, 4, 2, 1):
        probe = at + (step - 1)
        seen = take(tiles[0], probe)
        for number in range(1, len(tiles)):
            seen = jnp.where(tile == number, take(tiles[number], probe), seen)
        at += jnp.where(seen <= place, step, 0)
    slot = tile * 128 + at
    slot_ref[...] = jnp.where(lane[:half] < KEEP, slot[:half], slot[half:])


def squeeze(full, slot):
    half = slot.shape[0]
    lane = lax.broadcasted_iota(jnp.int32, (half, 128), 1)
    tile, at = slot // 128, slot % 128
    out = jnp.zeros((half, 128), jnp.float32)
    for number, part in enumerate(tiles_of(full)):
        got = jnp.where(lane < KEEP, take(part[:half], at), take(part[half:], at))
        out = jnp.where(tile == number, got, out)
    return out


def spread(packed, rank):
    half = packed.shape[0]
    parts = []
    for number, place in enumerate(tiles_of(rank)):
        at = jnp.maximum(place, 0)
        got = jnp.concatenate([take(packed, at[:half]), take(packed, at[half:] + KEEP)], axis=0)
        parts.append(jnp.where(place >= 0, got, 0.0))
    return jnp.concatenate(parts, axis=1)


def term_kernel(acts_ref, cots_ref, enc_ref, dec_ref, slot_ref, out_ref):
    blocks, _, rows, width = acts_ref.shape
    half = rows // 2
    acts = acts_ref[...].reshape(blocks * rows, width)
    pre = jnp.dot(acts, enc_ref[...], preferred_element_type=jnp.float32)
    cots = cots_ref[...].reshape(blocks * rows, width)
    cot = lax.dot_general(cots, dec_ref[...], (((1,), (1,)), ((), ())), preferred_element_type=jnp.float32)
    for block in range(blocks):
        slot = slot_ref[block * half : (block + 1) * half, :]
        at = slice(block * rows, (block + 1) * rows)
        out_ref[block, :half] = squeeze(pre[at], slot).astype(out_ref.dtype)
        out_ref[block, half:] = squeeze(cot[at], slot).astype(out_ref.dtype)


def sum_kernel(place_ref, terms_ref, slot_ref, bias_ref, out_ref):
    total = jnp.sum(terms_ref[...].astype(jnp.float32), axis=0)
    half = slot_ref.shape[0]
    bias = jnp.broadcast_to(bias_ref[...], (2 * half, bias_ref.shape[1]))
    code = total[:half] + squeeze(bias, slot_ref[...])
    both = jnp.concatenate([code, total[half:]], axis=0).astype(out_ref.dtype)
    out_ref[...] = jnp.broadcast_to(both[None], out_ref.shape)


def grad_kernel(sums_ref, rank_ref, acts_ref, cots_ref, enc_ref, dec_ref, bias_ref, code_ref, pre_ref):
    blocks, pair, _ = sums_ref.shape
    half = pair // 2
    tokens = rank_ref.shape[0]

    @pl.when(pl.program_id(0) == 0)
    def _():
        total = jnp.zeros(bias_ref.shape, jnp.float32)
        for block in range(blocks):
            at = slice(block * pair, (block + 1) * pair)
            rank = rank_ref[at, :]
            packed = sums_ref[block].astype(jnp.float32)
            code_ref[at, :] = spread(packed[:half], rank).astype(code_ref.dtype)
            pre = spread(packed[half:], rank)
            pre_ref[at, :] = pre.astype(pre_ref.dtype)
            total += jnp.sum(pre, axis=0, keepdims=True)
        bias_ref[...] = total

    over_tokens = (((0,), (0,)), ((), ()))
    cots = cots_ref[...].reshape(tokens, -1)
    dec = lax.dot_general(code_ref[...], cots, over_tokens, preferred_element_type=jnp.float32)
    dec_ref[...] = dec.astype(dec_ref.dtype)
    acts = acts_ref[...].reshape(tokens, -1)
    enc = lax.dot_general(acts, pre_ref[...], over_tokens, preferred_element_type=jnp.float32)
    enc_ref[...] = enc.astype(enc_ref.dtype)


def params():
    return pltpu.CompilerParams(vmem_limit_bytes=VMEM)


def local(activations, cotangents, enc_weight, dec_weight, enc_bias, active_mask):
    tokens, latents = active_mask.shape
    rows, width = activations.shape[1:]
    blocks = tokens // rows
    half = rows // 2
    layers = blocks
    f32, bf16 = jnp.float32, jnp.bfloat16

    own = jnp.stack([activations[0], cotangents[0]])
    both = lax.all_gather(own, "latent", axis=0, tiled=False)

    rank, slot = pl.pallas_call(
        rank_kernel,
        grid=(blocks,),
        in_specs=[pl.BlockSpec((rows, latents), lambda i: (i, 0))],
        out_specs=[pl.BlockSpec((rows, latents), lambda i: (i, 0)), pl.BlockSpec((half, 128), lambda i: (i, 0))],
        out_shape=[
            jax.ShapeDtypeStruct((tokens, latents), jnp.int32),
            jax.ShapeDtypeStruct((tokens // 2, 128), jnp.int32),
        ],
        compiler_params=params(),
        cost_estimate=pl.CostEstimate(flops=8 * 10**9, bytes_accessed=5 * 10**6, transcendentals=0),
        name="ranks",
    )(active_mask)

    group = 4
    terms = pl.pallas_call(
        term_kernel,
        grid=(blocks // group,),
        in_specs=[
            pl.BlockSpec((group, 1, rows, width), lambda i: (i, 0, 0, 0)),
            pl.BlockSpec((group, 1, rows, width), lambda i: (i, 1, 0, 0)),
            pl.BlockSpec((width, latents), lambda i: (0, 0)),
            pl.BlockSpec((latents, width), lambda i: (0, 0)),
            pl.BlockSpec((group * half, 128), lambda i: (i, 0)),
        ],
        out_specs=pl.BlockSpec((group, 2 * half, 128), lambda i: (i, 0, 0)),
        out_shape=jax.ShapeDtypeStruct((blocks, 2 * half, 128), bf16),
        compiler_params=params(),
        name="terms",
    )(both, both, enc_weight[0], dec_weight[0], slot)

    mine = lax.all_to_all(terms, "layer", 0, 0)
    place = lax.axis_index("layer").astype(jnp.int32)[None]
    sums = pl.pallas_call(
        sum_kernel,
        grid_spec=pltpu.PrefetchScalarGridSpec(
            num_scalar_prefetch=1,
            grid=(1,),
            in_specs=[
                pl.BlockSpec((layers, 2 * half, 128), lambda i, place: (0, 0, 0)),
                pl.BlockSpec((half, 128), lambda i, place: (place[0], 0)),
                pl.BlockSpec((1, latents), lambda i, place: (0, 0)),
            ],
            out_specs=pl.BlockSpec((layers, 2 * half, 128), lambda i, place: (0, 0, 0)),
        ),
        out_shape=jax.ShapeDtypeStruct((layers, 2 * half, 128), bf16),
        compiler_params=params(),
        name="sums",
    )(place, mine, slot, enc_bias[None, :])
    sums = lax.all_to_all(sums, "layer", 0, 0)

    cut = 256
    enc_grad, dec_grad, bias_grad = pl.pallas_call(
        grad_kernel,
        grid=(width // cut,),
        in_specs=[
            pl.BlockSpec((blocks, 2 * half, 128), lambda i: (0, 0, 0)),
            pl.BlockSpec((tokens, latents), lambda i: (0, 0)),
            pl.BlockSpec((blocks, 1, rows, cut), lambda i: (0, 0, 0, i)),
            pl.BlockSpec((blocks, 1, rows, cut), lambda i: (0, 1, 0, i)),
        ],
        out_specs=[
            pl.BlockSpec((cut, latents), lambda i: (i, 0)),
            pl.BlockSpec((latents, cut), lambda i: (0, i)),
            pl.BlockSpec((1, latents), lambda i: (0, 0)),
        ],
        out_shape=[
            jax.ShapeDtypeStruct((width, latents), bf16),
            jax.ShapeDtypeStruct((latents, width), bf16),
            jax.ShapeDtypeStruct((1, latents), f32),
        ],
        scratch_shapes=[pltpu.VMEM((tokens, latents), bf16), pltpu.VMEM((tokens, latents), bf16)],
        compiler_params=params(),
        name="grads",
    )(sums, rank, both, both)
    return enc_grad[None], dec_grad[None], bias_grad[0]


def solution(mesh):
    return jax.shard_map(
        local,
        mesh=mesh,
        in_specs=(
            P("layer", "latent", None),
            P("layer", "latent", None),
            P("layer", None, "latent"),
            P("layer", "latent", None),
            P("latent"),
            P(None, "latent"),
        ),
        out_specs=(P("layer", None, "latent"), P("layer", "latent", None), P("latent")),
        check_vma=False,
    )
```

time: 335 us -> 141 us (0.42)
  waiting for transfers between devices: 290 us -> 57.4 us
  Pallas kernels: 0 us -> 39.3 us
  matrix products: 23.5 us -> 0 us
  blocking collectives: 0 us -> 17 us
  starting transfers between devices: 0.11 us -> 8.67 us
    psum x1 -> x0, waiting for transfers between devices: 209 us -> none  [local(): code_cot = lax.psum(cot_terms, 'layer')]
    pallas_call x0 -> x4, Pallas kernels: none -> 39.3 us  [the longest x1 15.5 us: local(): pl.pallas_call(rank_kernel, grid=(blocks,), in_specs=[pl.BlockSpec((rows,...]
    all_gather x2 -> x1, waiting for transfers between devices: 79.8 us -> 43.5 us  [local(): both = lax.all_gather(own, 'latent', axis=0, tiled=False)]
    dot_general x4 -> x0, matrix products: 23.5 us -> none  [the longest x1 7.34 us: local(): lax.dot_general(code, whole_cots, (((0,), (0,)), ((), ())), preferred_ele...]
    all_to_all x0 -> x1, blocking collectives: none -> 17 us  [local(): sums = lax.all_to_all(sums, 'layer', 0, 0)]
    all_to_all x0 -> x1, waiting for transfers between devices: none -> 13.9 us  [local(): mine = lax.all_to_all(terms, 'layer', 0, 0)]
    all_to_all x0 -> x1, starting transfers between devices: none -> 8.63 us  [local(): mine = lax.all_to_all(terms, 'layer', 0, 0)]
    reduce_sum x1 -> x0, other arithmetic: 3.51 us -> none  [local(): bias_grad = jnp.sum(pre_cot.astype(jnp.float32), axis=0)]
  transfers between devices with their start and end apart: 3 -> 2, of which waited for: 3 -> 2; matrix products, arithmetic and copies ran while one was open for 2% -> 0% of each run, Pallas kernels for 0% -> 11%
where the time goes in v1:
time: 141 us; the launch traced here: 139 us
  waiting for transfers between devices  57.4 us (41%)
  Pallas kernels  39.3 us (28%)
  blocking collectives  17 us (12%)
  between operations  14 us (10%)
  starting transfers between devices  8.67 us (6%)
  other arithmetic  1.87 us (1%)
    all_gather x1, waiting for transfers between devices, local(): both = lax.all_gather(own, 'latent', axis=0, tiled=False)  43.5 us
    all_to_all x1, blocking collectives, local(): sums = lax.all_to_all(sums, 'layer', 0, 0)  17 us
    pallas_call x1, Pallas kernels, local(): pl.pallas_call(rank_kernel, grid=(blocks,), in_specs=[pl.BlockSpec((rows,...  15.5 us
    all_to_all x1, waiting for transfers between devices, local(): mine = lax.all_to_all(terms, 'layer', 0, 0)  13.9 us
    pallas_call x1, Pallas kernels, local(): pl.pallas_call(grad_kernel, grid=(width // cut,), in_specs=[pl.BlockSpec(...  12.7 us
    pallas_call x1, Pallas kernels, local(): pl.pallas_call(term_kernel, grid=(blocks // group,), in_specs=[pl.BlockSp...  9.33 us
    all_to_all x1, starting transfers between devices, local(): mine = lax.all_to_all(terms, 'layer', 0, 0)  8.63 us
  transfers between devices with their start and end apart: 2, of which 2 were waited for; matrix products, arithmetic and copies ran while one was open for 0% of the time, Pallas kernels for 11%

profile of v1, /device:TPU:2, one launch (start us, length us, event | category | flops | bytes accessed | tf_op | source)
XLA Modules:
  0.0 139.0 jit_solution(15324442761745086249)
XLA Ops:
  7.2 0.0 all-gather.3.cloned.1.call-start
  7.2 1.9 %pad_maximum_fusion = bf16[2,64,2048]{2,1,0:T(8,128)(2,1)} fusion(bf16[1,64,2048]{2,1,0:T(8,128)(2,1)} %param.7, bf16[1,64,2048]{2,1,0:T(8,128)(2,1)} %param.6), kind=kLoop, calls=%fused_computation | loop fusion | flops 262144 | bytes 1048576 | tf_op jit(solution)/shard_map/stack | solution.py:130
  9.1 0.0 all-gather.3.cloned.1.call-update
  9.1 15.5 %ranks.1 = (s32[1024,512]{1,0:T(8,128)}, s32[512,128]{1,0:T(8,128)}) custom-call(s32[1024,512]{1,0:T(8,128)} %mask_ref.1), custom_call_target="tpu_custom_call" | custom-call | flops 8000000000 | bytes 5000000 | tf_op jit(solution)/shard_map/ranks/pallas_call | solution.py:133
  24.6 43.5 %all-gather.3.cloned.1.call-done = bf16[32,64,2048]{2,1,0:T(8,128)(2,1)} async-done(((bf16[2,64,2048]{2,1,0:T(8,128)(2,1)}), bf16[32,64,2048]{2,1,0:T(8,128)(2,1)}) %all-gather.3.cloned.1.call-update) | async-done | bytes 8388624 | tf_op jit(solution)/shard_map/all_gather | solution.py:131
  68.1 9.3 %terms.1 = bf16[16,64,128]{2,1,0:T(8,128)(2,1)} custom-call(bf16[16,2,64,2048]{3,2,1,0:T(8,128)(2,1)} %bitcast.8, bf16[16,2,64,2048]{3,2,1,0:T(8,128)(2,1)} %bitcast.9, bf16[2048,512]{1,0:T(8,128)(2,1)} %bitcast.12, bf16[512,2048]{1,0:T(8,128)(2,1)} %bitcast.13, s32[512,128]{1,0:T(8,128)} %get-tuple-element.8.slot_ref), custom_call_target="tpu_custom_call" | custom-call | tf_op jit(solution)/shard_map/terms/pallas_call | solution.py:148
  77.4 8.6 %all-to-all-start = ((bf16[16,64,128]{2,1,0:T(8,128)(2,1)}), bf16[16,64,128]{2,1,0:T(8,128)(2,1)S(1)}, u32[]{:S(2)}, u32[]{:S(2)}) async-start(bf16[16,64,128]{2,1,0:T(8,128)(2,1)} %terms.1), calls=%async_computation | async-start | bytes 524288 | tf_op jit(solution)/shard_map/all_to_all | solution.py:164
  86.1 13.9 %all-to-all-done.terms_ref = bf16[16,64,128]{2,1,0:T(8,128)(2,1)S(1)} async-done(((bf16[16,64,128]{2,1,0:T(8,128)(2,1)}), bf16[16,64,128]{2,1,0:T(8,128)(2,1)S(1)}, u32[]{:S(2)}, u32[]{:S(2)}) %all-to-all-start) | async-done | bytes 262176 | tf_op jit(solution)/shard_map/all_to_all | solution.py:164
  99.9 0.0 copy-start
  99.9 0.7 copy-done
  100.6 1.8 %sums.1 = bf16[16,64,128]{2,1,0:T(8,128)(2,1)} custom-call(s32[1]{0:T(128)} %bitcast.place_ref, bf16[16,64,128]{2,1,0:T(8,128)(2,1)} %copy-done, s32[512,128]{1,0:T(8,128)} %get-tuple-element.8.slot_ref, f32[1,512]{1,0:T(1,128)} %bitcast.14), custom_call_target="tpu_custom_call" | custom-call | tf_op jit(solution)/shard_map/sums/pallas_call | solution.py:166
  102.4 17.0 %all_to_all.10.sums_ref = bf16[16,64,128]{2,1,0:T(8,128)(2,1)} all-to-all(bf16[16,64,128]{2,1,0:T(8,128)(2,1)} %sums.1), channel_id=1, replica_groups=mesh['layer'=16,'latent'=16] {'layer'}, dimensions={0} | all-to-all | bytes 524288 | tf_op jit(solution)/shard_map/all_to_all | solution.py:182
  119.4 12.7 %grads.1 = (bf16[2048,512]{1,0:T(8,128)(2,1)}, bf16[512,2048]{1,0:T(8,128)(2,1)}, f32[1,512]{1,0:T(1,128)}) custom-call(bf16[16,64,128]{2,1,0:T(8,128)(2,1)} %all_to_all.10.sums_ref, s32[1024,512]{1,0:T(8,128)} %get-tuple-element.9.rank_ref, bf16[16,2,64,2048]{3,2,1,0:T(8,128)(2,1)} %bitcast.10, bf16[16,2,64,2048]{3,2,1,0:T(8,128)(2,1)} %bitcast.11), custom_call_target="tpu_custom_call" | custom-call | tf_op jit(solution)/shard_map/grads/pallas_call | solution.py:185
Async XLA Ops:
  7.2 60.9 %all-gather.3.cloned.1.call-start = ((), (), s32[]{:S(2)}) async-start(), calls=%async_computation.2 | async-start | bytes 8912896 | tf_op jit(solution)/shard_map/all_gather | solution.py:131
  77.4 22.5 %all-to-all-start = ((bf16[16,64,128]{2,1,0:T(8,128)(2,1)}), bf16[16,64,128]{2,1,0:T(8,128)(2,1)S(1)}, u32[]{:S(2)}, u32[]{:S(2)}) async-start(bf16[16,64,128]{2,1,0:T(8,128)(2,1)} %terms.1), calls=%async_computation | async-start | bytes 524288 | tf_op jit(solution)/shard_map/all_to_all | solution.py:164
  99.9 0.7 copy-start
Sparse Core Ops, SparseCore 0:
  10.4 57.6 all-gather.2

commit v2 on v0

v2 whole, which is shorter than its diff:
```python
import functools

import jax
import jax.numpy as jnp
from jax import lax
from jax.experimental import pallas as pl
from jax.experimental.pallas import tpu as pltpu
from jax.sharding import PartitionSpec as P

KEEP = 64


def take(values, lanes):
    return jnp.take_along_axis(values, lanes, axis=1, mode="promise_in_bounds")


def tiles_of(array):
    return [array[:, at : at + 128] for at in range(0, array.shape[1], 128)]


def rank_kernel(order_ref, mask_ref, rank_ref, slot_ref):
    latents = mask_ref.shape[1]
    blocks = order_ref.shape[0]
    rows = mask_ref.shape[0] // blocks
    half = rows // 2
    f32, bf16, i32 = jnp.float32, jnp.bfloat16, jnp.int32
    shape = (latents, latents)
    row, column = lax.broadcasted_iota(i32, shape, 0), lax.broadcasted_iota(i32, shape, 1)
    upper = (row <= column).astype(f32).astype(bf16)
    row, column = row[:, :128], column[:, :128]
    ahead = (row < 16 * column).astype(f32).astype(bf16)
    bits = jnp.where(row // 16 == column, jnp.left_shift(1, row % 16), 0).astype(f32).astype(bf16)
    group = 4
    for first in range(0, blocks, group):
        mask = [mask_ref[pl.ds(pl.multiple_of(order_ref[first + k] * rows, rows), rows), :] for k in range(group)]
        mask = jnp.concatenate(mask, axis=0)
        ones = mask.astype(f32).astype(bf16)
        count = jnp.dot(ones, upper, preferred_element_type=f32).astype(i32)
        rank_ref[first * rows : (first + group) * rows, :] = jnp.where(mask > 0, count - 1, -1)
        before = jnp.dot(ones, ahead, preferred_element_type=f32).astype(i32)
        word = jnp.dot(ones, bits, preferred_element_type=f32).astype(i32)
        lane = lax.broadcasted_iota(i32, (group * rows, 128), 1)
        place = lane % KEEP
        segment = jnp.zeros(lane.shape, i32)
        base = jnp.zeros(lane.shape, i32)
        for step in (16, 8, 4, 2, 1):
            seen = take(before, segment + step)
            segment += jnp.where(seen <= place, step, 0)
            base = jnp.where(seen <= place, seen, base)
        word = take(word, segment)
        left = place - base
        at = segment * 16
        for step in (8, 4, 2, 1):
            low = word & ((1 << step) - 1)
            ones = low
            if step > 1:
                ones = (ones & 0x5555) + ((ones >> 1) & 0x5555)
            if step > 2:
                ones = (ones & 0x3333) + ((ones >> 2) & 0x3333)
            if step > 4:
                ones = (ones & 0x0F0F) + ((ones >> 4) & 0x0F0F)
            past = left >= ones
            left = jnp.where(past, left - ones, left)
            word = jnp.where(past, word >> step, low)
            at += jnp.where(past, step, 0)
        for k in range(group):
            one, two = at[k * rows : k * rows + half], at[k * rows + half : (k + 1) * rows]
            to = (first + k) * half
            slot_ref[to : to + half, :] = jnp.where(lane[:half] < KEEP, one, two)


def squeeze(full, slot):
    half = slot.shape[0]
    lane = lax.broadcasted_iota(jnp.int32, (half, 128), 1)
    tile, at = slot // 128, slot % 128
    out = jnp.zeros((half, 128), jnp.float32)
    for number, part in enumerate(tiles_of(full)):
        got = jnp.where(lane < KEEP, take(part[:half], at), take(part[half:], at))
        out = jnp.where(tile == number, got, out)
    return out


def spread(packed, rank):
    half = packed.shape[0]
    parts = []
    for number, place in enumerate(tiles_of(rank)):
        at = jnp.maximum(place, 0)
        got = jnp.concatenate([take(packed, at[:half]), take(packed, at[half:] + KEEP)], axis=0)
        parts.append(jnp.where(place >= 0, got, 0.0))
    return jnp.concatenate(parts, axis=1)


def read(pieces, places, columns=slice(None)):
    parts = [pieces[n][:, columns] if lead is None else pieces[n][lead, :, columns] for n, lead in places]
    return jnp.concatenate(parts, axis=0)


def term_kernel(acts_at, cots_at, first, earlier, *refs):
    out_ref = refs[-1]
    given = refs[len(refs) - 1 - earlier : -1]
    pieces = refs[: len(refs) - 4 - earlier]
    enc_ref, dec_ref, slot_ref = refs[len(pieces) : len(pieces) + 3]
    chunk = 0
    for ref in given:
        out_ref[chunk : chunk + ref.shape[0]] = ref[...]
        chunk += ref.shape[0]
    pre = jnp.dot(read(pieces, acts_at), enc_ref[...], preferred_element_type=jnp.float32)
    cot = lax.dot_general(
        read(pieces, cots_at), dec_ref[...], (((1,), (1,)), ((), ())), preferred_element_type=jnp.float32
    )
    rows, half = 64, 32
    tokens = pre.shape[0]
    for block in range(tokens // rows):
        slot = slot_ref[first // 2 + block * half : first // 2 + (block + 1) * half, :]
        at = slice(block * rows, (block + 1) * rows)
        to = slice(block % 2 * half, (block % 2 + 1) * half)
        out_ref[chunk + block // 2, to, :] = squeeze(pre[at], slot).astype(out_ref.dtype)
        out_ref[chunk + tokens // 128 + block // 2, to, :] = squeeze(cot[at], slot).astype(out_ref.dtype)


def sum_kernel(place_ref, terms_ref, slot_ref, bias_ref, out_ref):
    total = jnp.sum(terms_ref[...].astype(jnp.float32), axis=0)
    half = total.shape[0]
    bias = jnp.broadcast_to(bias_ref[...], (2 * half, bias_ref.shape[1]))
    slot = slot_ref[pl.ds(pl.multiple_of(place_ref[0] * half, half), half), :]
    total += jnp.where(place_ref[1] > 0, squeeze(bias, slot), 0.0)
    out_ref[...] = jnp.broadcast_to(total.astype(out_ref.dtype)[None], out_ref.shape)


def grad_kernel(acts_at, cots_at, sizes, *refs):
    sums_ref, rank_ref = refs[:2]
    pieces = refs[2:-8]
    enc_ref, dec_ref, bias_ref, code_ref, pre_ref, enc_tile, dec_tile, sems = refs[-8:]
    total = jnp.zeros(bias_ref.shape, jnp.float32)
    chunk = token = 0
    for size in sizes:
        for block in range(size // 64):
            rank = rank_ref[token : token + 64, :]
            at = slice(block % 2 * 32, (block % 2 + 1) * 32)
            code = sums_ref[chunk + block // 2, at, :].astype(jnp.float32)
            code_ref[token : token + 64, :] = spread(code, rank).astype(code_ref.dtype)
            pre = sums_ref[chunk + size // 128 + block // 2, at, :].astype(jnp.float32)
            pre = spread(pre, rank)
            pre_ref[token : token + 64, :] = pre.astype(pre_ref.dtype)
            total += jnp.sum(pre, axis=0, keepdims=True)
            token += 64
        chunk += size // 64
    bias_ref[...] = total

    cut = enc_tile.shape[1]
    over_tokens = (((0,), (0,)), ((), ()))
    out = [[], []]
    for step in range(enc_ref.shape[0] // cut):
        columns = slice(step * cut, (step + 1) * cut)
        side = step % 2
        for copy in out[side]:
            copy.wait()
        dec = lax.dot_general(
            code_ref[...], read(pieces, cots_at, columns), over_tokens, preferred_element_type=jnp.float32
        )
        dec_tile[side] = dec.astype(dec_tile.dtype)
        enc = lax.dot_general(
            read(pieces, acts_at, columns), pre_ref[...], over_tokens, preferred_element_type=jnp.float32
        )
        enc_tile[side] = enc.astype(enc_tile.dtype)
        out[side] = [
            pltpu.make_async_copy(dec_tile.at[side], dec_ref.at[:, columns], sems.at[0, side]),
            pltpu.make_async_copy(enc_tile.at[side], enc_ref.at[columns, :], sems.at[1, side]),
        ]
        for copy in out[side]:
            copy.start()
    for copy in out[0] + out[1]:
        copy.wait()


def params(mib):
    return pltpu.CompilerParams(vmem_limit_bytes=mib * 1024 * 1024)


def whole():
    return pl.BlockSpec(memory_space=pltpu.VMEM)


def device(x, y, core):
    return (x * 4 + y) * 2 + core


def hop(dx, dy, dcore):
    return [
        (device(x, y, core), device((x + dx) % 2, (y + dy) % 4, (core + dcore) % 2))
        for x in range(2)
        for y in range(4)
        for core in range(2)
    ]


def east(values):
    return lax.ppermute(values, "latent", hop(1, 0, 0))


def up(values):
    return lax.ppermute(values, "latent", hop(0, 1, 0))


def down(values):
    return lax.ppermute(values, "latent", hop(0, -1, 0))


def twin(values):
    return lax.ppermute(values, "latent", hop(0, 0, 1))


ORIGINS = [
    (dx, dy, core)
    for dx, dy in ((0, 0), (1, 0), (0, 3), (0, 1), (0, 2), (1, 3), (1, 1), (1, 2))
    for core in (0, 1)
]


def stack_kernel(first_ref, second_ref, out_ref):
    out_ref[0] = first_ref[...]
    out_ref[1] = second_ref[...]


def local(activations, cotangents, enc_weight, dec_weight, enc_bias, active_mask):
    tokens, latents = active_mask.shape
    rows, width = activations.shape[1:]
    blocks = tokens // rows
    half = rows // 2
    f32, bf16 = jnp.float32, jnp.bfloat16
    acts, cots = activations[0], cotangents[0]
    enc, dec = enc_weight[0], dec_weight[0]

    here = lax.axis_index("latent").astype(jnp.int32)
    x, y, core = here // 8, here // 2 % 4, here % 2
    far_x, far_y, far_core = (jnp.array(column, jnp.int32) for column in zip(*ORIGINS))
    order = device((x + far_x) % 2, (y + far_y) % 4, (core + far_core) % 2)
    layer = lax.axis_index("layer").astype(jnp.int32)
    is_code = (layer < 4) | ((layer >= 8) & (layer < 11)) | (layer == 14)
    block = jnp.where(layer < 4, layer, jnp.where(layer < 11, layer - 4, 7))
    block = jnp.where(is_code, block, 0)
    place = jnp.stack([block, is_code.astype(jnp.int32)])
    smem = pl.BlockSpec(memory_space=pltpu.SMEM)

    own = pl.pallas_call(
        stack_kernel,
        in_specs=[whole(), whole()],
        out_specs=whole(),
        out_shape=jax.ShapeDtypeStruct((2, rows, width), bf16),
        compiler_params=params(4),
        name="stack",
    )(acts, cots)
    rank, slot = pl.pallas_call(
        rank_kernel,
        in_specs=[smem, whole()],
        out_specs=[whole(), whole()],
        out_shape=[
            jax.ShapeDtypeStruct((tokens, latents), jnp.int32),
            jax.ShapeDtypeStruct((tokens // 2, 128), jnp.int32),
        ],
        compiler_params=params(12),
        cost_estimate=pl.CostEstimate(flops=3 * 10**9, bytes_accessed=4 * 10**6, transcendentals=0),
        name="ranks",
    )(order, active_mask)

    a_x = east(acts)
    low, high = up(own), down(own)
    c_x = east(cots)
    a_x_low, a_x_high = up(a_x), down(a_x)
    low, high, rank, slot, place = lax.optimization_barrier((low, high, rank, slot, place))
    far_1, far_2 = up(low[:, :half]), down(high[:, half:])
    c_x_low, c_x_high = east(low[1]), east(high[1])
    a_x_far_1, a_x_far_2 = up(a_x_low[:half]), down(a_x_high[half:])
    far_1, far_2, own = lax.optimization_barrier((far_1, far_2, own))
    c_x_far = east(jnp.concatenate([far_1[1], far_2[1]]))

    pieces = [own, a_x, c_x, low, high]
    pieces += [far_1, far_2, a_x_low, a_x_high, c_x_low, c_x_high]
    pieces += [a_x_far_1, a_x_far_2, c_x_far]
    doubled = [piece for one in pieces for piece in (one, twin(one))]
    sizes = (512, 384, 128)
    acts_at = [
        [[(0, 0)], [(1, None)], [(3, 0)], [(4, 0)]],
        [[(5, 0), (6, 0)], [(7, None)], [(8, None)]],
        [[(11, None), (12, None)]],
    ]
    cots_at = [
        [[(0, 1)], [(2, None)], [(3, 1)], [(4, 1)]],
        [[(5, 1), (6, 1)], [(9, None)], [(10, None)]],
        [[(13, None)]],
    ]

    def with_twins(items, first=0):
        return [(2 * (n - first) + core, lead) for item in items for core in (0, 1) for n, lead in item]

    terms = []
    spans = ((0, 5), (5, 11), (11, 14))
    for number, (first, last) in enumerate(spans):
        size, start = sizes[number], sum(sizes[:number])
        used = doubled[2 * first : 2 * last]
        at = with_twins(acts_at[number], first), with_twins(cots_at[number], first)
        earlier = terms if number == 2 else []
        given = sum(array.shape[0] for array in earlier)
        kernel = functools.partial(term_kernel, *at, start, len(earlier))
        out = pl.pallas_call(
            kernel,
            in_specs=[whole()] * (len(used) + 3 + len(earlier)),
            out_specs=whole(),
            out_shape=jax.ShapeDtypeStruct((given + size // 64, 64, 128), bf16),
            compiler_params=params(12),
            cost_estimate=pl.CostEstimate(
                flops=4 * size * width * latents, bytes_accessed=4 * size * width, transcendentals=0
            ),
            name=("near", "middle", "far")[number],
        )(*used, enc, dec, slot, *earlier)
        terms = terms + [out]

    mine = lax.all_to_all(terms[2], "layer", 0, 0)
    sums = pl.pallas_call(
        sum_kernel,
        in_specs=[smem, whole(), whole(), whole()],
        out_specs=whole(),
        out_shape=jax.ShapeDtypeStruct((blocks, rows, 128), bf16),
        compiler_params=params(4),
        name="sums",
    )(place, mine, slot, enc_bias[None, :])
    sums = lax.all_to_all(sums, "layer", 0, 0)

    cut = 256
    all_acts = [at for items in acts_at for at in with_twins(items)]
    all_cots = [at for items in cots_at for at in with_twins(items)]
    hbm = pl.BlockSpec(memory_space=pl.ANY)
    enc_grad, dec_grad, bias_grad = pl.pallas_call(
        functools.partial(grad_kernel, all_acts, all_cots, sizes),
        in_specs=[whole()] * (2 + len(doubled)),
        out_specs=[hbm, hbm, whole()],
        out_shape=[
            jax.ShapeDtypeStruct((width, latents), bf16),
            jax.ShapeDtypeStruct((latents, width), bf16),
            jax.ShapeDtypeStruct((1, latents), f32),
        ],
        scratch_shapes=[
            pltpu.VMEM((tokens, latents), bf16),
            pltpu.VMEM((tokens, latents), bf16),
            pltpu.VMEM((2, cut, latents), bf16),
            pltpu.VMEM((2, latents, cut), bf16),
            pltpu.SemaphoreType.DMA((2, 2)),
        ],
        compiler_params=params(16),
        name="grads",
    )(sums, rank, *doubled)
    return enc_grad[None], dec_grad[None], bias_grad[0]


def solution(mesh):
    return jax.shard_map(
        local,
        mesh=mesh,
        in_specs=(
            P("layer", "latent", None),
            P("layer", "latent", None),
            P("layer", None, "latent"),
            P("layer", "latent", None),
            P("latent"),
            P(None, "latent"),
        ),
        out_specs=(P("layer", None, "latent"), P("layer", "latent", None), P("latent")),
        check_vma=False,
    )
```

time: 335 us -> 112 us (0.33)
  waiting for transfers between devices: 290 us -> 31.7 us
  blocking collectives: 0 us -> 39.2 us
  matrix products: 23.5 us -> 0 us
  Pallas kernels: 0 us -> 19.2 us
  starting transfers between devices: 0.11 us -> 16 us
  between operations: 13.8 us -> 0.98 us
    psum x1 -> x0, waiting for transfers between devices: 209 us -> none  [local(): code_cot = lax.psum(cot_terms, 'layer')]
    all_gather x2 -> x0, waiting for transfers between devices: 79.8 us -> none  [the longest x1 43.8 us: local(): whole_cots = lax.all_gather(cotangents[0], 'latent', axis=0, tiled=True)]
    all_to_all x0 -> x2, blocking collectives: none -> 39.2 us  [the longest x1 23.6 us: local(): mine = lax.all_to_all(terms[2], 'layer', 0, 0)]
    ppermute x0 -> x27, waiting for transfers between devices: none -> 31.7 us  [the longest x4 11.3 us: up(): return lax.ppermute(values, 'latent', hop(0, 1, 0))]
    dot_general x4 -> x0, matrix products: 23.5 us -> none  [the longest x1 7.34 us: local(): lax.dot_general(code, whole_cots, (((0,), (0,)), ((), ())), preferred_ele...]
    pallas_call x0 -> x7, Pallas kernels: none -> 19.2 us  [the longest x1 9.07 us: local(): pl.pallas_call(functools.partial(grad_kernel, all_acts, all_cots, sizes),...]
    ppermute x0 -> x27, starting transfers between devices: none -> 16 us  [the longest x4 8.26 us: down(): return lax.ppermute(values, 'latent', hop(0, -1, 0))]
    reduce_sum x1 -> x0, other arithmetic: 3.51 us -> none  [local(): bias_grad = jnp.sum(pre_cot.astype(jnp.float32), axis=0)]
  transfers between devices with their start and end apart: 3 -> 27, of which waited for: 3 -> 12; matrix products, arithmetic and copies ran while one was open for 2% -> 1% of each run, Pallas kernels for 0% -> 7%
where the time goes in v2:
time: 112 us; the launch traced here: 111 us
  blocking collectives  39.2 us (35%)
  waiting for transfers between devices  31.7 us (28%)
  Pallas kernels  19.2 us (17%)
  starting transfers between devices  16 us (14%)
  local copies, waits for them, and re-layouts  3.61 us (3%)
    all_to_all x1, blocking collectives, local(): mine = lax.all_to_all(terms[2], 'layer', 0, 0)  23.6 us
    all_to_all x1, blocking collectives, local(): sums = lax.all_to_all(sums, 'layer', 0, 0)  15.5 us
    ppermute x4, waiting for transfers between devices, up(): return lax.ppermute(values, 'latent', hop(0, 1, 0))  11.3 us
    ppermute x4, waiting for transfers between devices, down(): return lax.ppermute(values, 'latent', hop(0, -1, 0))  9.66 us
    ppermute x5, waiting for transfers between devices, east(): return lax.ppermute(values, 'latent', hop(1, 0, 0))  9.62 us
    pallas_call x1, Pallas kernels, local(): pl.pallas_call(functools.partial(grad_kernel, all_acts, all_cots, sizes),...  9.07 us
    ppermute x4, starting transfers between devices, down(): return lax.ppermute(values, 'latent', hop(0, -1, 0))  8.26 us
    pallas_call x3, Pallas kernels, local(): pl.pallas_call(kernel, in_specs=[whole()] * (len(used) + 3 + len(earlier)...  5.7 us
  transfers between devices with their start and end apart: 27, of which 12 were waited for; matrix products, arithmetic and copies ran while one was open for 1% of the time, Pallas kernels for 7%

profile of v2, /device:TPU:2, one launch (start us, length us, event | category | flops | bytes accessed | tf_op | source)
XLA Modules:
  0.0 111.5 jit_solution(1159655727575532487)
XLA Ops:
  0.6 2.4 %collective-permute-start.2 = (bf16[64,2048]{1,0:T(8,128)(2,1)}, bf16[64,2048]{1,0:T(8,128)(2,1)S(1)}, u32[]{:S(2)}, u32[]{:S(2)}) collective-permute-start(bf16[64,2048]{1,0:T(8,128)(2,1)} %bitcast.24), channel_id=1, source_target_pairs={{0,8},{1,9},{2,10},{3,11},{4,12},{5,13},{6,14},{7,15},{8,0},{9,1},... | collective-permute-start | bytes 786440 | tf_op jit(solution)/shard_map/ppermute | solution.py:198
  5.0 2.7 %collective-permute-start.1 = (bf16[2,64,2048]{2,1,0:T(8,128)(2,1)S(1)}, bf16[2,64,2048]{2,1,0:T(8,128)(2,1)S(1)}, u32[]{:S(2)}, u32[]{:S(2)}) collective-permute-start(bf16[2,64,2048]{2,1,0:T(8,128)(2,1)S(1)} %stack.18.refs_0_.refs_2_), channel_id=1, source_target_pairs={{0,6},{1,7},{2,0},{3,1},{4,2},{5,3},{6,4},{7,5},{8,14},{9,15},{10,... | collective-permute-start | bytes 1572872 | tf_op jit(solution)/shard_map/ppermute | solution.py:206
  8.6 1.6 %copy-done.5 = s32[1024,512]{1,0:T(8,128)S(1)} copy-done((s32[1024,512]{1,0:T(8,128)S(1)}, s32[1024,512]{1,0:T(8,128)}, u32[]{:S(2)}) %copy-start.5) | copy-done | bytes 2097176
  10.2 3.7 %ranks.1 = (s32[1024,512]{1,0:T(8,128)S(1)}, s32[512,128]{1,0:T(8,128)S(1)}) custom-call(s32[16]{0:T(128)S(1)} %fusion.1.order_ref, s32[1024,512]{1,0:T(8,128)S(1)} %copy-done.5), custom_call_target="tpu_custom_call" | custom-call | flops 3000000000 | bytes 4000000 | tf_op jit(solution)/shard_map/ranks/pallas_call | solution.py:253
  14.0 3.3 %collective-permute-start.6 = (bf16[64,2048]{1,0:T(8,128)(2,1)S(1)}, bf16[64,2048]{1,0:T(8,128)(2,1)S(1)}, u32[]{:S(2)}, u32[]{:S(2)}) collective-permute-start(bf16[64,2048]{1,0:T(8,128)(2,1)S(1)} %collective-permute-done.2.refs_2_.refs_4_), channel_id=1, source_target_pairs={{0,6},{1,7},{2,0},{3,1},{4,2},{5,3},{6,4},{7,5},{8,14},{9,15},{10,... | collective-permute-start | bytes 786440 | tf_op jit(solution)/shard_map/ppermute | solution.py:206
  17.3 1.6 %collective-permute-done.1.refs_8_.refs_10_ = bf16[2,64,2048]{2,1,0:T(8,128)(2,1)S(1)} collective-permute-done((bf16[2,64,2048]{2,1,0:T(8,128)(2,1)S(1)}, bf16[2,64,2048]{2,1,0:T(8,128)(2,1)S(1)}, u32[]{:S(2)}, u32[]{:S(2)}) %collective-permute-start.1) | collective-permute-done | bytes 524320 | tf_op jit(solution)/shard_map/ppermute | solution.py:206
  18.9 3.4 %collective-permute-done.refs_6_.refs_8_ = bf16[2,64,2048]{2,1,0:T(8,128)(2,1)S(1)} collective-permute-done((bf16[2,64,2048]{2,1,0:T(8,128)(2,1)S(1)}, bf16[2,64,2048]{2,1,0:T(8,128)(2,1)S(1)}, u32[]{:S(2)}, u32[]{:S(2)}) %collective-permute-start) | collective-permute-done | bytes 524320 | tf_op jit(solution)/shard_map/ppermute | solution.py:202
  22.7 1.8 %collective-permute-done.6.refs_6_.refs_18_ = bf16[64,2048]{1,0:T(8,128)(2,1)S(1)} collective-permute-done((bf16[64,2048]{1,0:T(8,128)(2,1)S(1)}, bf16[64,2048]{1,0:T(8,128)(2,1)S(1)}, u32[]{:S(2)}, u32[]{:S(2)}) %collective-permute-start.6) | collective-permute-done | bytes 262176 | tf_op jit(solution)/shard_map/ppermute | solution.py:206
  24.5 1.1 collective-permute-start.9
  25.7 4.0 %collective-permute-done.10.refs_2_.refs_14_ = bf16[2,32,2048]{2,1,0:T(8,128)(2,1)S(1)} collective-permute-done((bf16[2,32,2048]{2,1,0:T(8,128)(2,1)S(1)}, bf16[2,32,2048]{2,1,0:T(8,128)(2,1)S(1)}, u32[]{:S(2)}, u32[]{:S(2)}) %collective-permute-start.10) | collective-permute-done | bytes 262176 | tf_op jit(solution)/shard_map/ppermute | solution.py:206
  30.2 3.6 %collective-permute-done.9.refs_0_.refs_12_ = bf16[2,32,2048]{2,1,0:T(8,128)(2,1)S(1)} collective-permute-done((bf16[2,32,2048]{2,1,0:T(8,128)(2,1)S(1)}, bf16[2,32,2048]{2,1,0:T(8,128)(2,1)S(1)}, u32[]{:S(2)}, u32[]{:S(2)}) %collective-permute-start.9) | collective-permute-done | bytes 262176 | tf_op jit(solution)/shard_map/ppermute | solution.py:202
  33.8 1.8 %collective-permute-start.7 = (bf16[32,2048]{1,0:T(8,128)(2,1)S(1)}, bf16[32,2048]{1,0:T(8,128)(2,1)S(1)}, u32[]{:S(2)}, u32[]{:S(2)}) collective-permute-start(bf16[32,2048]{1,0:T(8,128)(2,1)S(1)} %slice.33), channel_id=1, source_target_pairs={{0,6},{1,7},{2,0},{3,1},{4,2},{5,3},{6,4},{7,5},{8,14},{9,15},{10,... | collective-permute-start | bytes 393224 | tf_op jit(solution)/shard_map/ppermute | solution.py:206
  36.2 1.3 %collective-permute-done.25.refs_10_.refs_22_ = bf16[64,2048]{1,0:T(8,128)(2,1)S(1)} collective-permute-done((bf16[64,2048]{1,0:T(8,128)(2,1)S(1)}, bf16[64,2048]{1,0:T(8,128)(2,1)S(1)}, u32[]{:S(2)}, u32[]{:S(2)}) %collective-permute-start.25) | collective-permute-done | bytes 262176 | tf_op jit(solution)/shard_map/ppermute | solution.py:198
  37.5 2.3 %collective-permute-done.7.refs_2_.refs_26_ = bf16[32,2048]{1,0:T(8,128)(2,1)S(1)} collective-permute-done((bf16[32,2048]{1,0:T(8,128)(2,1)S(1)}, bf16[32,2048]{1,0:T(8,128)(2,1)S(1)}, u32[]{:S(2)}, u32[]{:S(2)}) %collective-permute-start.7) | collective-permute-done | bytes 131104 | tf_op jit(solution)/shard_map/ppermute | solution.py:206
  40.9 3.9 %collective-permute-done.23.refs_8_.refs_20_ = bf16[64,2048]{1,0:T(8,128)(2,1)S(1)} collective-permute-done((bf16[64,2048]{1,0:T(8,128)(2,1)S(1)}, bf16[64,2048]{1,0:T(8,128)(2,1)S(1)}, u32[]{:S(2)}, u32[]{:S(2)}) %collective-permute-start.23) | collective-permute-done | bytes 262176 | tf_op jit(solution)/shard_map/ppermute | solution.py:198
  45.3 4.4 %collective-permute-done.11.refs_4_.refs_28_ = bf16[64,2048]{1,0:T(8,128)(2,1)S(1)} collective-permute-done((bf16[64,2048]{1,0:T(8,128)(2,1)S(1)}, bf16[64,2048]{1,0:T(8,128)(2,1)S(1)}, u32[]{:S(2)}, u32[]{:S(2)}) %collective-permute-start.11) | collective-permute-done | bytes 262176 | tf_op jit(solution)/shard_map/ppermute | solution.py:198
  50.2 1.0 collective-permute-done.20.refs_3_.refs_15_
  51.8 1.9 %middle.1.refs_10_ = bf16[6,64,128]{2,1,0:T(8,128)(2,1)S(1)} custom-call(bf16[2,32,2048]{2,1,0:T(8,128)(2,1)S(1)} %collective-permute-done.9.refs_0_.refs_12_, bf16[2,32,2048]{2,1,0:T(8,128)(2,1)S(1)} %collective-permute-done.19.refs_1_.refs_13_, bf16[2,32,2048]{2,1,0:T(8,128)(2,1)S(1)} %collective-permute-done.10.refs_2_.refs_14_, ...), custom_call_target="tpu_custom_call" | custom-call | flops 1610612736 | bytes 3145728 | tf_op jit(solution)/shard_map/middle/pallas_call | solution.py:305
  53.7 4.3 %collective-permute-done.4.refs_0_.refs_24_ = bf16[32,2048]{1,0:T(8,128)(2,1)S(1)} collective-permute-done((bf16[32,2048]{1,0:T(8,128)(2,1)S(1)}, bf16[32,2048]{1,0:T(8,128)(2,1)S(1)}, u32[]{:S(2)}, u32[]{:S(2)}) %collective-permute-start.4) | collective-permute-done | bytes 131104 | tf_op jit(solution)/shard_map/ppermute | solution.py:202
  58.5 2.5 %near.1.refs_9_ = bf16[8,64,128]{2,1,0:T(8,128)(2,1)S(1)} custom-call(bf16[2,64,2048]{2,1,0:T(8,128)(2,1)S(1)} %stack.18.refs_0_.refs_2_, bf16[2,64,2048]{2,1,0:T(8,128)(2,1)S(1)} %collective-permute-done.13.refs_1_.refs_3_, bf16[64,2048]{1,0:T(8,128)(2,1)S(1)} %collective-permute-done.2.refs_2_.refs_4_, ...), custom_call_target="tpu_custom_call" | custom-call | flops 2147483648 | bytes 4194304 | tf_op jit(solution)/shard_map/near/pallas_call | solution.py:305
  61.1 1.2 %far.1 = bf16[16,64,128]{2,1,0:T(8,128)(2,1)S(1)} custom-call(bf16[32,2048]{1,0:T(8,128)(2,1)S(1)} %collective-permute-done.4.refs_0_.refs_24_, bf16[32,2048]{1,0:T(8,128)(2,1)S(1)} %collective-permute-done.5.refs_1_.refs_25_, bf16[32,2048]{1,0:T(8,128)(2,1)S(1)} %collective-permute-done.7.refs_2_.refs_26_, ...), custom_call_target="tpu_custom_call" | custom-call | flops 536870912 | bytes 1048576 | tf_op jit(solution)/shard_map/far/pallas_call | solution.py:305
  62.3 23.6 %all_to_all.10.terms_ref = bf16[16,64,128]{2,1,0:T(8,128)(2,1)S(1)} all-to-all(bf16[16,64,128]{2,1,0:T(8,128)(2,1)S(1)} %far.1), channel_id=1, replica_groups=mesh['layer'=16,'latent'=16] {'layer'}, dimensions={0} | all-to-all | bytes 524288 | tf_op jit(solution)/shard_map/all_to_all | solution.py:318
  86.7 15.5 %all_to_all.11.refs_0_ = bf16[16,64,128]{2,1,0:T(8,128)(2,1)S(1)} all-to-all(bf16[16,64,128]{2,1,0:T(8,128)(2,1)S(1)} %sums.1), channel_id=1, replica_groups=mesh['layer'=16,'latent'=16] {'layer'}, dimensions={0} | all-to-all | bytes 524288 | tf_op jit(solution)/shard_map/all_to_all | solution.py:327
  102.2 9.1 %grads.1 = (bf16[2048,512]{1,0:T(8,128)(2,1)}, bf16[512,2048]{1,0:T(8,128)(2,1)}, f32[1,512]{1,0:T(1,128)}) custom-call(bf16[16,64,128]{2,1,0:T(8,128)(2,1)S(1)} %all_to_all.11.refs_0_, s32[1024,512]{1,0:T(8,128)S(1)} %get-tuple-element.25.refs_1_, bf16[2,64,2048]{2,1,0:T(8,128)(2,1)S(1)} %stack.18.refs_0_.refs_2_, ...), custom_call_target="tpu_custom_call" | custom-call | tf_op jit(solution)/shard_map/grads/pallas_call | solution.py:333
  (61 shorter events, 8.3 us)
Async XLA Ops:
  0.6 13.2 %collective-permute-start.2 = (bf16[64,2048]{1,0:T(8,128)(2,1)}, bf16[64,2048]{1,0:T(8,128)(2,1)S(1)}, u32[]{:S(2)}, u32[]{:S(2)}) collective-permute-start(bf16[64,2048]{1,0:T(8,128)(2,1)} %bitcast.24), channel_id=1, source_target_pairs={{0,8},{1,9},{2,10},{3,11},{4,12},{5,13},{6,14},{7,15},{8,0},{9,1},... | collective-permute-start | bytes 786440 | tf_op jit(solution)/shard_map/ppermute | solution.py:198
  3.0 14.3 %collective-permute-start.15 = (bf16[64,2048]{1,0:T(8,128)(2,1)}, bf16[64,2048]{1,0:T(8,128)(2,1)S(1)}, u32[]{:S(2)}, u32[]{:S(2)}) collective-permute-start(bf16[64,2048]{1,0:T(8,128)(2,1)} %bitcast.26), channel_id=1, source_target_pairs={{0,8},{1,9},{2,10},{3,11},{4,12},{5,13},{6,14},{7,15},{8,0},{9,1},... | collective-permute-start | bytes 786440 | tf_op jit(solution)/shard_map/ppermute | solution.py:198
  5.0 13.9 %collective-permute-start.1 = (bf16[2,64,2048]{2,1,0:T(8,128)(2,1)S(1)}, bf16[2,64,2048]{2,1,0:T(8,128)(2,1)S(1)}, u32[]{:S(2)}, u32[]{:S(2)}) collective-permute-start(bf16[2,64,2048]{2,1,0:T(8,128)(2,1)S(1)} %stack.18.refs_0_.refs_2_), channel_id=1, source_target_pairs={{0,6},{1,7},{2,0},{3,1},{4,2},{5,3},{6,4},{7,5},{8,14},{9,15},{10,... | collective-permute-start | bytes 1572872 | tf_op jit(solution)/shard_map/ppermute | solution.py:206
  7.8 14.5 %collective-permute-start = (bf16[2,64,2048]{2,1,0:T(8,128)(2,1)S(1)}, bf16[2,64,2048]{2,1,0:T(8,128)(2,1)S(1)}, u32[]{:S(2)}, u32[]{:S(2)}) collective-permute-start(bf16[2,64,2048]{2,1,0:T(8,128)(2,1)S(1)} %stack.18.refs_0_.refs_2_), channel_id=1, source_target_pairs={{0,2},{1,3},{2,4},{3,5},{4,6},{5,7},{6,0},{7,1},{8,10},{9,11},{10,... | collective-permute-start | bytes 1572872 | tf_op jit(solution)/shard_map/ppermute | solution.py:202
  13.9 20.0 %collective-permute-start.14 = (bf16[64,2048]{1,0:T(8,128)(2,1)S(1)}, bf16[64,2048]{1,0:T(8,128)(2,1)S(1)}, u32[]{:S(2)}, u32[]{:S(2)}) collective-permute-start(bf16[64,2048]{1,0:T(8,128)(2,1)S(1)} %collective-permute-done.2.refs_2_.refs_4_), channel_id=1, source_target_pairs={{0,1},{1,0},{2,3},{3,2},{4,5},{5,4},{6,7},{7,6},{8,9},{9,8},{10,11... | collective-permute-start | bytes 786440 | tf_op jit(solution)/shard_map/ppermute | solution.py:210
  14.0 10.5 %collective-permute-start.6 = (bf16[64,2048]{1,0:T(8,128)(2,1)S(1)}, bf16[64,2048]{1,0:T(8,128)(2,1)S(1)}, u32[]{:S(2)}, u32[]{:S(2)}) collective-permute-start(bf16[64,2048]{1,0:T(8,128)(2,1)S(1)} %collective-permute-done.2.refs_2_.refs_4_), channel_id=1, source_target_pairs={{0,6},{1,7},{2,0},{3,1},{4,2},{5,3},{6,4},{7,5},{8,14},{9,15},{10,... | collective-permute-start | bytes 786440 | tf_op jit(solution)/shard_map/ppermute | solution.py:206
  17.3 18.4 %collective-permute-start.3 = (bf16[64,2048]{1,0:T(8,128)(2,1)S(1)}, bf16[64,2048]{1,0:T(8,128)(2,1)S(1)}, u32[]{:S(2)}, u32[]{:S(2)}) collective-permute-start(bf16[64,2048]{1,0:T(8,128)(2,1)S(1)} %collective-permute-done.2.refs_2_.refs_4_), channel_id=1, source_target_pairs={{0,2},{1,3},{2,4},{3,5},{4,6},{5,7},{6,0},{7,1},{8,10},{9,11},{10,... | collective-permute-start | bytes 786440 | tf_op jit(solution)/shard_map/ppermute | solution.py:202
  18.9 17.3 %collective-permute-start.16 = (bf16[64,2048]{1,0:T(8,128)(2,1)S(1)}, bf16[64,2048]{1,0:T(8,128)(2,1)S(1)}, u32[]{:S(2)}, u32[]{:S(2)}) collective-permute-start(bf16[64,2048]{1,0:T(8,128)(2,1)S(1)} %collective-permute-done.15.refs_4_.refs_6_), channel_id=1, source_target_pairs={{0,1},{1,0},{2,3},{3,2},{4,5},{5,4},{6,7},{7,6},{8,9},{9,8},{10,11... | collective-permute-start | bytes 786440 | tf_op jit(solution)/shard_map/ppermute | solution.py:210
  22.3 7.3 %collective-permute-start.10 = (bf16[2,32,2048]{2,1,0:T(8,128)(2,1)S(1)}, bf16[2,32,2048]{2,1,0:T(8,128)(2,1)S(1)}, u32[]{:S(2)}, u32[]{:S(2)}) collective-permute-start(bf16[2,32,2048]{2,1,0:T(8,128)(2,1)S(1)} %slice.27), channel_id=1, source_target_pairs={{0,6},{1,7},{2,0},{3,1},{4,2},{5,3},{6,4},{7,5},{8,14},{9,15},{10,... | collective-permute-start | bytes 786440 | tf_op jit(solution)/shard_map/ppermute | solution.py:206
  24.5 9.3 %collective-permute-start.9 = (bf16[2,32,2048]{2,1,0:T(8,128)(2,1)S(1)}, bf16[2,32,2048]{2,1,0:T(8,128)(2,1)S(1)}, u32[]{:S(2)}, u32[]{:S(2)}) collective-permute-start(bf16[2,32,2048]{2,1,0:T(8,128)(2,1)S(1)} %slice.26), channel_id=1, source_target_pairs={{0,2},{1,3},{2,4},{3,5},{4,6},{5,7},{6,0},{7,1},{8,10},{9,11},{10,... | collective-permute-start | bytes 786440 | tf_op jit(solution)/shard_map/ppermute | solution.py:202
  29.6 7.8 %collective-permute-start.25 = (bf16[64,2048]{1,0:T(8,128)(2,1)S(1)}, bf16[64,2048]{1,0:T(8,128)(2,1)S(1)}, u32[]{:S(2)}, u32[]{:S(2)}) collective-permute-start(bf16[64,2048]{1,0:T(8,128)(2,1)S(1)} %slice_bitcast_fusion), channel_id=1, source_target_pairs={{0,8},{1,9},{2,10},{3,11},{4,12},{5,13},{6,14},{7,15},{8,0},{9,1},... | collective-permute-start | bytes 786440 | tf_op jit(solution)/shard_map/ppermute | solution.py:198
  33.8 6.5 %collective-permute-start.22 = (bf16[64,2048]{1,0:T(8,128)(2,1)S(1)}, bf16[64,2048]{1,0:T(8,128)(2,1)S(1)}, u32[]{:S(2)}, u32[]{:S(2)}) collective-permute-start(bf16[64,2048]{1,0:T(8,128)(2,1)S(1)} %collective-permute-done.6.refs_6_.refs_18_), channel_id=1, source_target_pairs={{0,1},{1,0},{2,3},{3,2},{4,5},{5,4},{6,7},{7,6},{8,9},{9,8},{10,11... | collective-permute-start | bytes 786440 | tf_op jit(solution)/shard_map/ppermute | solution.py:210
  33.8 6.0 %collective-permute-start.7 = (bf16[32,2048]{1,0:T(8,128)(2,1)S(1)}, bf16[32,2048]{1,0:T(8,128)(2,1)S(1)}, u32[]{:S(2)}, u32[]{:S(2)}) collective-permute-start(bf16[32,2048]{1,0:T(8,128)(2,1)S(1)} %slice.33), channel_id=1, source_target_pairs={{0,6},{1,7},{2,0},{3,1},{4,2},{5,3},{6,4},{7,5},{8,14},{9,15},{10,... | collective-permute-start | bytes 393224 | tf_op jit(solution)/shard_map/ppermute | solution.py:206
  35.7 9.1 %collective-permute-start.23 = (bf16[64,2048]{1,0:T(8,128)(2,1)S(1)}, bf16[64,2048]{1,0:T(8,128)(2,1)S(1)}, u32[]{:S(2)}, u32[]{:S(2)}) collective-permute-start(bf16[64,2048]{1,0:T(8,128)(2,1)S(1)} %slice_bitcast_fusion.1), channel_id=1, source_target_pairs={{0,8},{1,9},{2,10},{3,11},{4,12},{5,13},{6,14},{7,15},{8,0},{9,1},... | collective-permute-start | bytes 786440 | tf_op jit(solution)/shard_map/ppermute | solution.py:198
  36.2 4.2 %collective-permute-start.21 = (bf16[64,2048]{1,0:T(8,128)(2,1)S(1)}, bf16[64,2048]{1,0:T(8,128)(2,1)S(1)}, u32[]{:S(2)}, u32[]{:S(2)}) collective-permute-start(bf16[64,2048]{1,0:T(8,128)(2,1)S(1)} %collective-permute-done.3.refs_4_.refs_16_), channel_id=1, source_target_pairs={{0,1},{1,0},{2,3},{3,2},{4,5},{5,4},{6,7},{7,6},{8,9},{9,8},{10,11... | collective-permute-start | bytes 786440 | tf_op jit(solution)/shard_map/ppermute | solution.py:210
  37.5 7.3 %collective-permute-start.26 = (bf16[64,2048]{1,0:T(8,128)(2,1)S(1)}, bf16[64,2048]{1,0:T(8,128)(2,1)S(1)}, u32[]{:S(2)}, u32[]{:S(2)}) collective-permute-start(bf16[64,2048]{1,0:T(8,128)(2,1)S(1)} %collective-permute-done.25.refs_10_.refs_22_), channel_id=1, source_target_pairs={{0,1},{1,0},{2,3},{3,2},{4,5},{5,4},{6,7},{7,6},{8,9},{9,8},{10,11... | collective-permute-start | bytes 786440 | tf_op jit(solution)/shard_map/ppermute | solution.py:210
  39.8 9.9 %collective-permute-start.11 = (bf16[64,2048]{1,0:T(8,128)(2,1)S(1)}, bf16[64,2048]{1,0:T(8,128)(2,1)S(1)}, u32[]{:S(2)}, u32[]{:S(2)}) collective-permute-start(bf16[64,2048]{1,0:T(8,128)(2,1)S(1)} %pad_maximum_fusion), channel_id=1, source_target_pairs={{0,8},{1,9},{2,10},{3,11},{4,12},{5,13},{6,14},{7,15},{8,0},{9,1},... | collective-permute-start | bytes 786440 | tf_op jit(solution)/shard_map/ppermute | solution.py:198
  40.3 9.4 %collective-permute-start.19 = (bf16[2,32,2048]{2,1,0:T(8,128)(2,1)S(1)}, bf16[2,32,2048]{2,1,0:T(8,128)(2,1)S(1)}, u32[]{:S(2)}, u32[]{:S(2)}) collective-permute-start(bf16[2,32,2048]{2,1,0:T(8,128)(2,1)S(1)} %collective-permute-done.9.refs_0_.refs_12_), channel_id=1, source_target_pairs={{0,1},{1,0},{2,3},{3,2},{4,5},{5,4},{6,7},{7,6},{8,9},{9,8},{10,11... | collective-permute-start | bytes 786440 | tf_op jit(solution)/shard_map/ppermute | solution.py:210
  40.4 17.6 %collective-permute-start.17 = (bf16[2,64,2048]{2,1,0:T(8,128)(2,1)S(1)}, bf16[2,64,2048]{2,1,0:T(8,128)(2,1)S(1)}, u32[]{:S(2)}, u32[]{:S(2)}) collective-permute-start(bf16[2,64,2048]{2,1,0:T(8,128)(2,1)S(1)} %collective-permute-done.refs_6_.refs_8_), channel_id=1, source_target_pairs={{0,1},{1,0},{2,3},{3,2},{4,5},{5,4},{6,7},{7,6},{8,9},{9,8},{10,11... | collective-permute-start | bytes 1572872 | tf_op jit(solution)/shard_map/ppermute | solution.py:210
  44.8 13.7 %collective-permute-start.18 = (bf16[2,64,2048]{2,1,0:T(8,128)(2,1)S(1)}, bf16[2,64,2048]{2,1,0:T(8,128)(2,1)S(1)}, u32[]{:S(2)}, u32[]{:S(2)}) collective-permute-start(bf16[2,64,2048]{2,1,0:T(8,128)(2,1)S(1)} %collective-permute-done.1.refs_8_.refs_10_), channel_id=1, source_target_pairs={{0,1},{1,0},{2,3},{3,2},{4,5},{5,4},{6,7},{7,6},{8,9},{9,8},{10,11... | collective-permute-start | bytes 1572872 | tf_op jit(solution)/shard_map/ppermute | solution.py:210
  44.8 13.7 %collective-permute-start.13 = (bf16[2,64,2048]{2,1,0:T(8,128)(2,1)S(1)}, bf16[2,64,2048]{2,1,0:T(8,128)(2,1)S(1)}, u32[]{:S(2)}, u32[]{:S(2)}) collective-permute-start(bf16[2,64,2048]{2,1,0:T(8,128)(2,1)S(1)} %stack.18.refs_0_.refs_2_), channel_id=1, source_target_pairs={{0,1},{1,0},{2,3},{3,2},{4,5},{5,4},{6,7},{7,6},{8,9},{9,8},{10,11... | collective-permute-start | bytes 1572872 | tf_op jit(solution)/shard_map/ppermute | solution.py:210
  51.2 6.7 %collective-permute-start.4 = (bf16[32,2048]{1,0:T(8,128)(2,1)S(1)}, bf16[32,2048]{1,0:T(8,128)(2,1)S(1)}, u32[]{:S(2)}, u32[]{:S(2)}) collective-permute-start(bf16[32,2048]{1,0:T(8,128)(2,1)S(1)} %slice.32), channel_id=1, source_target_pairs={{0,2},{1,3},{2,4},{3,5},{4,6},{5,7},{6,0},{7,1},{8,10},{9,11},{10,... | collective-permute-start | bytes 393224 | tf_op jit(solution)/shard_map/ppermute | solution.py:202
  51.6 9.5 %collective-permute-start.12 = (bf16[64,2048]{1,0:T(8,128)(2,1)S(1)}, bf16[64,2048]{1,0:T(8,128)(2,1)S(1)}, u32[]{:S(2)}, u32[]{:S(2)}) collective-permute-start(bf16[64,2048]{1,0:T(8,128)(2,1)S(1)} %collective-permute-done.11.refs_4_.refs_28_), channel_id=1, source_target_pairs={{0,1},{1,0},{2,3},{3,2},{4,5},{5,4},{6,7},{7,6},{8,9},{9,8},{10,11... | collective-permute-start | bytes 786440 | tf_op jit(solution)/shard_map/ppermute | solution.py:210
  58.0 3.1 %collective-permute-start.5 = (bf16[32,2048]{1,0:T(8,128)(2,1)S(1)}, bf16[32,2048]{1,0:T(8,128)(2,1)S(1)}, u32[]{:S(2)}, u32[]{:S(2)}) collective-permute-start(bf16[32,2048]{1,0:T(8,128)(2,1)S(1)} %collective-permute-done.4.refs_0_.refs_24_), channel_id=1, source_target_pairs={{0,1},{1,0},{2,3},{3,2},{4,5},{5,4},{6,7},{7,6},{8,9},{9,8},{10,11... | collective-permute-start | bytes 393224 | tf_op jit(solution)/shard_map/ppermute | solution.py:210
  (9 other events, 114.4 us)

commit v3 on v2

--- a/solution.py
+++ b/solution.py
@@ -91,8 +91,7 @@
 
 
 def read(pieces, places, columns=slice(None)):
-    parts = [pieces[n][:, columns] if lead is None else pieces[n][lead, :, columns] for n, lead in places]
-    return jnp.concatenate(parts, axis=0)
+    return jnp.concatenate([pieces[n][first:last, columns] for n, first, last in places], axis=0)
 
 
 def term_kernel(acts_at, cots_at, first, earlier, *refs):
@@ -212,14 +211,52 @@
 
 ORIGINS = [
     (dx, dy, core)
-    for dx, dy in ((0, 0), (1, 0), (0, 3), (0, 1), (0, 2), (1, 3), (1, 1), (1, 2))
+    for dx, dy in ((0, 0), (1, 0), (0, 3), (0, 1), (1, 3), (1, 1), (0, 2), (1, 2))
     for core in (0, 1)
 ]
 
 
-def stack_kernel(first_ref, second_ref, out_ref):
-    out_ref[0] = first_ref[...]
-    out_ref[1] = second_ref[...]
+def pack_kernel(outs, *refs):
+    sems = refs[-1]
+    out_refs = refs[len(refs) - 1 - len(outs) : -1]
+    copies = []
+    for out_ref, parts in zip(out_refs, outs):
+        at = 0
+        for n, first, last in parts:
+            here = out_ref.at[at : at + last - first]
+            copies.append(pltpu.make_async_copy(refs[n].at[first:last], here, sems.at[len(copies)]))
+            at += last - first
+    for copy in copies:
+        copy.start()
+    for copy in copies:
+        copy.wait()
+
+
+def pack_all(*groups):
+    given, outs = [], []
+    for group in groups:
+        outs.append([])
+        for part in group:
+            array, first, last = part if isinstance(part, tuple) else (part, 0, part.shape[0])
+            outs[-1].append((len(given), first, last))
+            given.append(array)
+    width, dtype = given[0].shape[1], given[0].dtype
+    totals = [sum(last - first for _, first, last in parts) for parts in outs]
+    hbm = pl.BlockSpec(memory_space=pl.ANY)
+    return pl.pallas_call(
+        functools.partial(pack_kernel, outs),
+        in_specs=[hbm] * len(given),
+        out_specs=[hbm] * len(outs),
+        out_shape=[jax.ShapeDtypeStruct((total, width), dtype) for total in totals],
+        scratch_shapes=[pltpu.SemaphoreType.DMA((len(given),))],
+        compiler_params=params(2),
+        cost_estimate=pl.CostEstimate(flops=0, bytes_accessed=sum(totals) * 8192, transcendentals=0),
+        name="pack",
+    )(*given)
+
+
+def pack(*parts):
+    return pack_all(parts)[0]
 
 
 def local(activations, cotangents, enc_weight, dec_weight, enc_bias, active_mask):
@@ -236,20 +273,14 @@
     far_x, far_y, far_core = (jnp.array(column, jnp.int32) for column in zip(*ORIGINS))
     order = device((x + far_x) % 2, (y + far_y) % 4, (core + far_core) % 2)
     layer = lax.axis_index("layer").astype(jnp.int32)
-    is_code = (layer < 4) | ((layer >= 8) & (layer < 11)) | (layer == 14)
-    block = jnp.where(layer < 4, layer, jnp.where(layer < 11, layer - 4, 7))
+    is_code = (layer < 4) | ((layer >= 8) & (layer % 4 < 2))
+    block = jnp.where(layer < 8, layer, layer // 2 + layer % 2)
     block = jnp.where(is_code, block, 0)
     place = jnp.stack([block, is_code.astype(jnp.int32)])
     smem = pl.BlockSpec(memory_space=pltpu.SMEM)
 
-    own = pl.pallas_call(
-        stack_kernel,
-        in_specs=[whole(), whole()],
-        out_specs=whole(),
-        out_shape=jax.ShapeDtypeStruct((2, rows, width), bf16),
-        compiler_params=params(4),
-        name="stack",
-    )(acts, cots)
+    hbm = pl.BlockSpec(memory_space=pl.ANY)
+    tie = lax.optimization_barrier
     rank, slot = pl.pallas_call(
         rank_kernel,
         in_specs=[smem, whole()],
@@ -262,48 +293,46 @@
         cost_estimate=pl.CostEstimate(flops=3 * 10**9, bytes_accessed=4 * 10**6, transcendentals=0),
         name="ranks",
     )(order, active_mask)
-
     a_x = east(acts)
-    low, high = up(own), down(own)
-    c_x = east(cots)
-    a_x_low, a_x_high = up(a_x), down(a_x)
-    low, high, rank, slot, place = lax.optimization_barrier((low, high, rank, slot, place))
-    far_1, far_2 = up(low[:, :half]), down(high[:, half:])
-    c_x_low, c_x_high = east(low[1]), east(high[1])
-    a_x_far_1, a_x_far_2 = up(a_x_low[:half]), down(a_x_high[half:])
-    far_1, far_2, own = lax.optimization_barrier((far_1, far_2, own))
-    c_x_far = east(jnp.concatenate([far_1[1], far_2[1]]))
-
-    pieces = [own, a_x, c_x, low, high]
-    pieces += [far_1, far_2, a_x_low, a_x_high, c_x_low, c_x_high]
-    pieces += [a_x_far_1, a_x_far_2, c_x_far]
-    doubled = [piece for one in pieces for piece in (one, twin(one))]
-    sizes = (512, 384, 128)
+    c_low, c_high = up(cots), down(cots)
+    a_low, a_high = up(acts), down(acts)
+    a_x, cots_later = tie((a_x, cots))
+    c_x = east(cots_later)
+    c_x_near = east(pack(c_low, c_high))
+    sent = pack_all([a_x, (c_low, 0, half)], [a_x, (c_high, half, rows)])
+    *sent, a_low, a_high, rank, slot, place = tie((*sent, a_low, a_high, rank, slot, place))
+    third_low, third_high = up(sent[0]), down(sent[1])
+    sent = pack_all(
+        [(third_low, rows, rows + half), (third_high, rows, rows + half)],
+        [(a_low, 0, half), (third_low, 0, half)],
+        [(a_high, half, rows), (third_high, half, rows)],
+    )
+    c_x_far, fourth_low, fourth_high = east(sent[0]), up(sent[1]), down(sent[2])
+
+    *first, _ = tie((acts, cots, a_x, c_low, c_high, a_low, a_high, c_x, c_x))
+    first = pack(*first)
+    second = pack(third_low, third_high, c_x_near)
+    sizes = (512, 256, 256)
     acts_at = [
-        [[(0, 0)], [(1, None)], [(3, 0)], [(4, 0)]],
-        [[(5, 0), (6, 0)], [(7, None)], [(8, None)]],
-        [[(11, None), (12, None)]],
+        [[(0, k * rows, (k + 1) * rows)] for k in (0, 2, 5, 6)],
+        [[(1, 0, 64)], [(1, 96, 160)]],
+        [[(2, 0, 32), (2, 64, 96)], [(2, 32, 64), (2, 96, 128)]],
     ]
     cots_at = [
-        [[(0, 1)], [(2, None)], [(3, 1)], [(4, 1)]],
-        [[(5, 1), (6, 1)], [(9, None)], [(10, None)]],
-        [[(13, None)]],
+        [[(0, k * rows, (k + 1) * rows)] for k in (1, 7, 3, 4)],
+        [[(1, 192, 256)], [(1, 256, 320)]],
+        [[(1, 64, 96), (1, 160, 192)], [(2, 128, 192)]],
     ]
 
     def with_twins(items, first=0):
-        return [(2 * (n - first) + core, lead) for item in items for core in (0, 1) for n, lead in item]
-
-    terms = []
-    spans = ((0, 5), (5, 11), (11, 14))
-    for number, (first, last) in enumerate(spans):
-        size, start = sizes[number], sum(sizes[:number])
-        used = doubled[2 * first : 2 * last]
-        at = with_twins(acts_at[number], first), with_twins(cots_at[number], first)
-        earlier = terms if number == 2 else []
+        return [(2 * (n - first) + core, *at) for item in items for core in (0, 1) for n, *at in item]
+
+    def terms_of(number, earlier, used):
+        size, start, first_piece = sizes[number], sum(sizes[:number]), min(number, 1)
+        at = with_twins(acts_at[number], first_piece), with_twins(cots_at[number], first_piece)
         given = sum(array.shape[0] for array in earlier)
-        kernel = functools.partial(term_kernel, *at, start, len(earlier))
-        out = pl.pallas_call(
-            kernel,
+        return pl.pallas_call(
+            functools.partial(term_kernel, *at, start, len(earlier)),
             in_specs=[whole()] * (len(used) + 3 + len(earlier)),
             out_specs=whole(),
             out_shape=jax.ShapeDtypeStruct((given + size // 64, 64, 128), bf16),
@@ -313,9 +342,17 @@
             ),
             name=("near", "middle", "far")[number],
         )(*used, enc, dec, slot, *earlier)
-        terms = terms + [out]
-
-    mine = lax.all_to_all(terms[2], "layer", 0, 0)
+
+    doubled = [first, twin(first)]
+    terms = terms_of(0, [], doubled)
+    doubled += [second, twin(second)]
+    terms = terms_of(1, [terms], doubled[2:])
+    *doubled, terms, fourth_low, fourth_high, c_x_far = tie((*doubled, terms, fourth_low, fourth_high, c_x_far))
+    last = pack(fourth_low, fourth_high, c_x_far)
+    doubled += [last, twin(last)]
+    terms = terms_of(2, [terms], doubled[2:])
+
+    mine = lax.all_to_all(terms, "layer", 0, 0)
     sums = pl.pallas_call(
         sum_kernel,
         in_specs=[smem, whole(), whole(), whole()],
@@ -329,11 +366,10 @@
     cut = 256
     all_acts = [at for items in acts_at for at in with_twins(items)]
     all_cots = [at for items in cots_at for at in with_twins(items)]
-    hbm = pl.BlockSpec(memory_space=pl.ANY)
     enc_grad, dec_grad, bias_grad = pl.pallas_call(
         functools.partial(grad_kernel, all_acts, all_cots, sizes),
         in_specs=[whole()] * (2 + len(doubled)),
-        out_specs=[hbm, hbm, whole()],
+        out_specs=[pl.BlockSpec(memory_space=pl.ANY)] * 2 + [whole()],
         out_shape=[
             jax.ShapeDtypeStruct((width, latents), bf16),
             jax.ShapeDtypeStruct((latents, width), bf16),

time: 112 us -> 101 us (0.902)
  waiting for transfers between devices: 31.7 us -> 20.9 us
  local copies, waits for them, and re-layouts: 3.61 us -> 1.62 us
  Pallas kernels: 19.2 us -> 21 us
    ppermute x4, waiting for transfers between devices: 9.66 us -> 0.01 us  [down(): return lax.ppermute(values, 'latent', hop(0, -1, 0))]
    ppermute x4, starting transfers between devices: 8.26 us -> 11.7 us  [down(): return lax.ppermute(values, 'latent', hop(0, -1, 0))]
    ppermute x5 -> x4, waiting for transfers between devices: 9.62 us -> 6.21 us  [east(): return lax.ppermute(values, 'latent', hop(1, 0, 0))]
    ppermute x14 -> x3, starting transfers between devices: 2.28 us -> 0.28 us  [twin(): return lax.ppermute(values, 'latent', hop(0, 0, 1))]
    unnamed x12, local copies, waits for them, and re-layouts: 3.5 us -> 1.62 us
    pallas_call x4 -> x9, Pallas kernels: 5.74 us -> 7.59 us  [the longest x3 5.28 us: terms_of(): pl.pallas_call(functools.partial(term_kernel, *at, start, len(earlier)),...]
    ppermute x14 -> x3, waiting for transfers between devices: 1.13 us -> 2.28 us  [twin(): return lax.ppermute(values, 'latent', hop(0, 0, 1))]
    ppermute x5 -> x4, starting transfers between devices: 4.04 us -> 2.97 us  [east(): return lax.ppermute(values, 'latent', hop(1, 0, 0))]
  transfers between devices with their start and end apart: 27 -> 15, of which waited for: 12 -> 7; matrix products, arithmetic and copies ran while one was open for 1% -> 1% of each run, Pallas kernels for 7% -> 10%
where the time goes in v3:
time: 101 us; the launch traced here: 100 us
  blocking collectives  39.6 us (39%)
  Pallas kernels  21 us (21%)
  waiting for transfers between devices  20.9 us (21%)
  starting transfers between devices  15.4 us (15%)
  local copies, waits for them, and re-layouts  1.62 us (2%)
  between operations  1.03 us (1%)
    all_to_all x1, blocking collectives, local(): mine = lax.all_to_all(terms, 'layer', 0, 0)  23.7 us
    all_to_all x1, blocking collectives, local(): sums = lax.all_to_all(sums, 'layer', 0, 0)  15.9 us
    ppermute x4, waiting for transfers between devices, up(): return lax.ppermute(values, 'latent', hop(0, 1, 0))  12.4 us
    ppermute x4, starting transfers between devices, down(): return lax.ppermute(values, 'latent', hop(0, -1, 0))  11.7 us
    pallas_call x1, Pallas kernels, local(): pl.pallas_call(functools.partial(grad_kernel, all_acts, all_cots, sizes),...  9.03 us
    ppermute x4, waiting for transfers between devices, east(): return lax.ppermute(values, 'latent', hop(1, 0, 0))  6.21 us
    pallas_call x3, Pallas kernels, terms_of(): pl.pallas_call(functools.partial(term_kernel, *at, start, len(earlier)),...  5.28 us
    pallas_call x1, Pallas kernels, local(): pl.pallas_call(rank_kernel, in_specs=[smem, whole()], out_specs=[whole(),...  3.7 us
  transfers between devices with their start and end apart: 15, of which 7 were waited for; matrix products, arithmetic and copies ran while one was open for 1% of the time, Pallas kernels for 10%

profile of v3, /device:TPU:2, one launch (start us, length us, event | category | flops | bytes accessed | tf_op | source)
XLA Modules:
  0.0 100.3 jit_solution(13001371206487602668)
XLA Ops:
  0.6 3.1 %collective-permute-start.4 = (bf16[64,2048]{1,0:T(8,128)(2,1)}, bf16[64,2048]{1,0:T(8,128)(2,1)S(1)}, u32[]{:S(2)}, u32[]{:S(2)}) collective-permute-start(bf16[64,2048]{1,0:T(8,128)(2,1)} %bitcast.16), channel_id=1, source_target_pairs={{0,6},{1,7},{2,0},{3,1},{4,2},{5,3},{6,4},{7,5},{8,14},{9,15},{10,... | collective-permute-start | bytes 786440 | tf_op jit(solution)/shard_map/ppermute | solution.py:205
  3.7 1.3 %collective-permute-start = (bf16[64,2048]{1,0:T(8,128)(2,1)}, bf16[64,2048]{1,0:T(8,128)(2,1)S(1)}, u32[]{:S(2)}, u32[]{:S(2)}) collective-permute-start(bf16[64,2048]{1,0:T(8,128)(2,1)} %bitcast.18), channel_id=1, source_target_pairs={{0,8},{1,9},{2,10},{3,11},{4,12},{5,13},{6,14},{7,15},{8,0},{9,1},... | collective-permute-start | bytes 786440 | tf_op jit(solution)/shard_map/ppermute | solution.py:197
  5.0 2.5 %collective-permute-start.2 = (bf16[64,2048]{1,0:T(8,128)(2,1)}, bf16[64,2048]{1,0:T(8,128)(2,1)S(1)}, u32[]{:S(2)}, u32[]{:S(2)}) collective-permute-start(bf16[64,2048]{1,0:T(8,128)(2,1)} %bitcast.20), channel_id=1, source_target_pairs={{0,6},{1,7},{2,0},{3,1},{4,2},{5,3},{6,4},{7,5},{8,14},{9,15},{10,... | collective-permute-start | bytes 786440 | tf_op jit(solution)/shard_map/ppermute | solution.py:205
  7.6 0.7 fusion.1.order_ref
  8.3 3.4 %collective-permute-done.refs_0_.refs_2_ = bf16[64,2048]{1,0:T(8,128)(2,1)S(1)} collective-permute-done((bf16[64,2048]{1,0:T(8,128)(2,1)}, bf16[64,2048]{1,0:T(8,128)(2,1)S(1)}, u32[]{:S(2)}, u32[]{:S(2)}) %collective-permute-start) | collective-permute-done | bytes 262176 | tf_op jit(solution)/shard_map/ppermute | solution.py:197
  12.2 1.6 %copy-done.5 = s32[1024,512]{1,0:T(8,128)S(1)} copy-done((s32[1024,512]{1,0:T(8,128)S(1)}, s32[1024,512]{1,0:T(8,128)}, u32[]{:S(2)}) %copy-start.5) | copy-done | bytes 2097176
  13.8 3.7 %ranks.1 = (s32[1024,512]{1,0:T(8,128)S(1)}, s32[512,128]{1,0:T(8,128)S(1)}) custom-call(s32[16]{0:T(128)S(1)} %fusion.1.order_ref, s32[1024,512]{1,0:T(8,128)S(1)} %copy-done.5), custom_call_target="tpu_custom_call" | custom-call | flops 3000000000 | bytes 4000000 | tf_op jit(solution)/shard_map/ranks/pallas_call | solution.py:284
  17.5 1.0 collective-permute-done.1.refs_1_.refs_3_.refs_0_
  19.4 0.6 collective-permute-start.9
  20.4 2.9 %collective-permute-start.8 = (bf16[96,2048]{1,0:T(8,128)(2,1)S(1)}, bf16[96,2048]{1,0:T(8,128)(2,1)S(1)}, u32[]{:S(2)}, u32[]{:S(2)}) collective-permute-start(bf16[96,2048]{1,0:T(8,128)(2,1)S(1)} %get-tuple-element.56), channel_id=1, source_target_pairs={{0,6},{1,7},{2,0},{3,1},{4,2},{5,3},{6,4},{7,5},{8,14},{9,15},{10,... | collective-permute-start | bytes 1179656 | tf_op jit(solution)/shard_map/ppermute | solution.py:205
  23.3 9.2 %collective-permute-done.7.refs_0_.refs_3_ = bf16[96,2048]{1,0:T(8,128)(2,1)S(1)} collective-permute-done((bf16[96,2048]{1,0:T(8,128)(2,1)S(1)}, bf16[96,2048]{1,0:T(8,128)(2,1)S(1)}, u32[]{:S(2)}, u32[]{:S(2)}) %collective-permute-start.7) | collective-permute-done | bytes 393248 | tf_op jit(solution)/shard_map/ppermute | solution.py:201
  32.5 1.3 %collective-permute-done.9.refs_2_ = bf16[128,2048]{1,0:T(8,128)(2,1)S(1)} collective-permute-done((bf16[128,2048]{1,0:T(8,128)(2,1)S(1)}, bf16[128,2048]{1,0:T(8,128)(2,1)S(1)}, u32[]{:S(2)}, u32[]{:S(2)}) %collective-permute-start.9) | collective-permute-done | bytes 524320 | tf_op jit(solution)/shard_map/ppermute | solution.py:197
  34.4 1.1 %pack.10 = (bf16[64,2048]{1,0:T(8,128)(2,1)S(1)}, bf16[64,2048]{1,0:T(8,128)(2,1)S(1)}, bf16[64,2048]{1,0:T(8,128)(2,1)S(1)}) custom-call(bf16[96,2048]{1,0:T(8,128)(2,1)S(1)} %collective-permute-done.7.refs_0_.refs_3_, bf16[96,2048]{1,0:T(8,128)(2,1)S(1)} %collective-permute-done.8.refs_1_.refs_5_, ...), custom_call_target="tpu_custom_call" | custom-call | bytes 1572864 | tf_op jit(solution)/shard_map/pack/pallas_call | solution.py:246
  35.6 3.2 %collective-permute-start.12 = (bf16[64,2048]{1,0:T(8,128)(2,1)S(1)}, bf16[64,2048]{1,0:T(8,128)(2,1)S(1)}, u32[]{:S(2)}, u32[]{:S(2)}) collective-permute-start(bf16[64,2048]{1,0:T(8,128)(2,1)S(1)} %get-tuple-element.59), channel_id=1, source_target_pairs={{0,6},{1,7},{2,0},{3,1},{4,2},{5,3},{6,4},{7,5},{8,14},{9,15},{10,... | collective-permute-start | bytes 786440 | tf_op jit(solution)/shard_map/ppermute | solution.py:205
  39.3 2.5 %near.1.refs_5_ = bf16[8,64,128]{2,1,0:T(8,128)(2,1)S(1)} custom-call(bf16[512,2048]{1,0:T(8,128)(2,1)S(1)} %pack.7.refs_0_.refs_2_, bf16[512,2048]{1,0:T(8,128)(2,1)S(1)} %collective-permute-done.6.refs_1_.refs_3_, bf16[2048,512]{1,0:T(8,128)(2,1)S(1)} %bitcast.10, bf16[512,2048]{1,0:T(8,128)(2,1)S(1)} %bitcast.13, ...), custom_call_target="tpu_custom_call" | custom-call | flops 2147483648 | bytes 4194304 | tf_op jit(solution)/shard_map/near/pallas_call | solution.py:334
  41.9 1.4 %middle.1.refs_7_ = bf16[12,64,128]{2,1,0:T(8,128)(2,1)S(1)} custom-call(bf16[320,2048]{1,0:T(8,128)(2,1)S(1)} %pack.9.refs_0_.refs_4_, bf16[320,2048]{1,0:T(8,128)(2,1)S(1)} %collective-permute-done.10.refs_1_.refs_5_, bf16[2048,512]{1,0:T(8,128)(2,1)S(1)} %bitcast.11, bf16[512,2048]{1,0:T(8,128)(2,1)S(1)} %bitcast.14, ...), custom_call_target="tpu_custom_call" | custom-call | flops 1073741824 | bytes 2097152 | tf_op jit(solution)/shard_map/middle/pallas_call | solution.py:334
  43.3 2.2 %collective-permute-done.11.refs_0_ = bf16[64,2048]{1,0:T(8,128)(2,1)S(1)} collective-permute-done((bf16[64,2048]{1,0:T(8,128)(2,1)S(1)}, bf16[64,2048]{1,0:T(8,128)(2,1)S(1)}, u32[]{:S(2)}, u32[]{:S(2)}) %collective-permute-start.11) | collective-permute-done | bytes 262176 | tf_op jit(solution)/shard_map/ppermute | solution.py:201
  45.4 1.5 %collective-permute-done.13.refs_2_ = bf16[64,2048]{1,0:T(8,128)(2,1)S(1)} collective-permute-done((bf16[64,2048]{1,0:T(8,128)(2,1)S(1)}, bf16[64,2048]{1,0:T(8,128)(2,1)S(1)}, u32[]{:S(2)}, u32[]{:S(2)}) %collective-permute-start.13) | collective-permute-done | bytes 262176 | tf_op jit(solution)/shard_map/ppermute | solution.py:197
  47.1 2.3 %collective-permute-done.14.refs_3_.refs_7_ = bf16[192,2048]{1,0:T(8,128)(2,1)S(1)} collective-permute-done((bf16[192,2048]{1,0:T(8,128)(2,1)S(1)}, bf16[192,2048]{1,0:T(8,128)(2,1)S(1)}, u32[]{:S(2)}, u32[]{:S(2)}) %collective-permute-start.14) | collective-permute-done | bytes 786464 | tf_op jit(solution)/shard_map/ppermute | solution.py:209
  49.4 1.4 %far.1 = bf16[16,64,128]{2,1,0:T(8,128)(2,1)S(1)} custom-call(bf16[320,2048]{1,0:T(8,128)(2,1)S(1)} %pack.9.refs_0_.refs_4_, bf16[320,2048]{1,0:T(8,128)(2,1)S(1)} %collective-permute-done.10.refs_1_.refs_5_, bf16[192,2048]{1,0:T(8,128)(2,1)S(1)} %pack.11.refs_2_.refs_6_, bf16[192,2048]{1,0:T(8,128)(2,1)S(1)} %collective-permute-done.14.refs_3_.refs_7_, ...), custom_call_target="tpu_custom_call" | custom-call | flops 1073741824 | bytes 2097152 | tf_op jit(solution)/shard_map/far/pallas_call | solution.py:334
  50.8 23.7 %all_to_all.10.terms_ref = bf16[16,64,128]{2,1,0:T(8,128)(2,1)S(1)} all-to-all(bf16[16,64,128]{2,1,0:T(8,128)(2,1)S(1)} %far.1), channel_id=1, replica_groups=mesh['layer'=16,'latent'=16] {'layer'}, dimensions={0} | all-to-all | bytes 524288 | tf_op jit(solution)/shard_map/all_to_all | solution.py:355
  74.5 0.7 sums.1
  75.2 15.9 %all_to_all.11.refs_0_ = bf16[16,64,128]{2,1,0:T(8,128)(2,1)S(1)} all-to-all(bf16[16,64,128]{2,1,0:T(8,128)(2,1)S(1)} %sums.1), channel_id=1, replica_groups=mesh['layer'=16,'latent'=16] {'layer'}, dimensions={0} | all-to-all | bytes 524288 | tf_op jit(solution)/shard_map/all_to_all | solution.py:364
  91.1 9.0 %grads.1 = (bf16[2048,512]{1,0:T(8,128)(2,1)}, bf16[512,2048]{1,0:T(8,128)(2,1)}, f32[1,512]{1,0:T(1,128)}) custom-call(bf16[16,64,128]{2,1,0:T(8,128)(2,1)S(1)} %all_to_all.11.refs_0_, s32[1024,512]{1,0:T(8,128)S(1)} %get-tuple-element.67.refs_1_, bf16[512,2048]{1,0:T(8,128)(2,1)S(1)} %pack.7.refs_0_.refs_2_, ...), custom_call_target="tpu_custom_call" | custom-call | tf_op jit(solution)/shard_map/grads/pallas_call | solution.py:369
  (34 shorter events, 3.1 us)
Async XLA Ops:
  0.6 18.3 %collective-permute-start.4 = (bf16[64,2048]{1,0:T(8,128)(2,1)}, bf16[64,2048]{1,0:T(8,128)(2,1)S(1)}, u32[]{:S(2)}, u32[]{:S(2)}) collective-permute-start(bf16[64,2048]{1,0:T(8,128)(2,1)} %bitcast.16), channel_id=1, source_target_pairs={{0,6},{1,7},{2,0},{3,1},{4,2},{5,3},{6,4},{7,5},{8,14},{9,15},{10,... | collective-permute-start | bytes 786440 | tf_op jit(solution)/shard_map/ppermute | solution.py:205
  3.7 15.2 %collective-permute-start.3 = (bf16[64,2048]{1,0:T(8,128)(2,1)}, bf16[64,2048]{1,0:T(8,128)(2,1)S(1)}, u32[]{:S(2)}, u32[]{:S(2)}) collective-permute-start(bf16[64,2048]{1,0:T(8,128)(2,1)} %bitcast.17), channel_id=1, source_target_pairs={{0,2},{1,3},{2,4},{3,5},{4,6},{5,7},{6,0},{7,1},{8,10},{9,11},{10,... | collective-permute-start | bytes 786440 | tf_op jit(solution)/shard_map/ppermute | solution.py:201
  3.7 8.0 %collective-permute-start = (bf16[64,2048]{1,0:T(8,128)(2,1)}, bf16[64,2048]{1,0:T(8,128)(2,1)S(1)}, u32[]{:S(2)}, u32[]{:S(2)}) collective-permute-start(bf16[64,2048]{1,0:T(8,128)(2,1)} %bitcast.18), channel_id=1, source_target_pairs={{0,8},{1,9},{2,10},{3,11},{4,12},{5,13},{6,14},{7,15},{8,0},{9,1},... | collective-permute-start | bytes 786440 | tf_op jit(solution)/shard_map/ppermute | solution.py:197
  5.0 12.5 %collective-permute-start.2 = (bf16[64,2048]{1,0:T(8,128)(2,1)}, bf16[64,2048]{1,0:T(8,128)(2,1)S(1)}, u32[]{:S(2)}, u32[]{:S(2)}) collective-permute-start(bf16[64,2048]{1,0:T(8,128)(2,1)} %bitcast.20), channel_id=1, source_target_pairs={{0,6},{1,7},{2,0},{3,1},{4,2},{5,3},{6,4},{7,5},{8,14},{9,15},{10,... | collective-permute-start | bytes 786440 | tf_op jit(solution)/shard_map/ppermute | solution.py:205
  7.5 11.0 %collective-permute-start.1 = (bf16[64,2048]{1,0:T(8,128)(2,1)}, bf16[64,2048]{1,0:T(8,128)(2,1)S(1)}, u32[]{:S(2)}, u32[]{:S(2)}) collective-permute-start(bf16[64,2048]{1,0:T(8,128)(2,1)} %bitcast.21), channel_id=1, source_target_pairs={{0,2},{1,3},{2,4},{3,5},{4,6},{5,7},{6,0},{7,1},{8,10},{9,11},{10,... | collective-permute-start | bytes 786440 | tf_op jit(solution)/shard_map/ppermute | solution.py:201
  8.3 10.7 %copy-start.2 = (bf16[1,64,2048]{2,1,0:T(8,128)(2,1)S(1)}, bf16[1,64,2048]{2,1,0:T(8,128)(2,1)}, u32[]{:S(2)}) copy-start(bf16[1,64,2048]{2,1,0:T(8,128)(2,1)} %param.9) | copy-start | bytes 786436
  8.3 10.7 %copy-start.3 = (bf16[1,64,2048]{2,1,0:T(8,128)(2,1)S(1)}, bf16[1,64,2048]{2,1,0:T(8,128)(2,1)}, u32[]{:S(2)}) copy-start(bf16[1,64,2048]{2,1,0:T(8,128)(2,1)} %param.10) | copy-start | bytes 786436
  11.7 7.3 %collective-permute-start.5 = (bf16[64,2048]{1,0:T(8,128)(2,1)}, bf16[64,2048]{1,0:T(8,128)(2,1)S(1)}, u32[]{:S(2)}, u32[]{:S(2)}) collective-permute-start(bf16[64,2048]{1,0:T(8,128)(2,1)} %bitcast.22), channel_id=1, source_target_pairs={{0,8},{1,9},{2,10},{3,11},{4,12},{5,13},{6,14},{7,15},{8,0},{9,1},... | collective-permute-start | bytes 786440 | tf_op jit(solution)/shard_map/ppermute | solution.py:197
  12.2 1.6 %copy-start.5 = (s32[1024,512]{1,0:T(8,128)S(1)}, s32[1024,512]{1,0:T(8,128)}, u32[]{:S(2)}) copy-start(s32[1024,512]{1,0:T(8,128)} %mask_ref.1) | copy-start | bytes 6291460
  19.2 20.1 %collective-permute-start.6 = (bf16[512,2048]{1,0:T(8,128)(2,1)S(1)}, bf16[512,2048]{1,0:T(8,128)(2,1)S(1)}, u32[]{:S(2)}, u32[]{:S(2)}) collective-permute-start(bf16[512,2048]{1,0:T(8,128)(2,1)S(1)} %pack.7.refs_0_.refs_2_), channel_id=1, source_target_pairs={{0,1},{1,0},{2,3},{3,2},{4,5},{5,4},{6,7},{7,6},{8,9},{9,8},{10,11... | collective-permute-start | bytes 6291464 | tf_op jit(solution)/shard_map/ppermute | solution.py:209
  19.4 19.9 %copy-start = (bf16[1,2048,512]{2,1,0:T(8,128)(2,1)S(1)}, bf16[1,2048,512]{2,1,0:T(8,128)(2,1)}, u32[]{:S(2)}) copy-start(bf16[1,2048,512]{2,1,0:T(8,128)(2,1)} %param.11) | copy-start | bytes 6291460
  19.4 19.9 %copy-start.1 = (bf16[1,512,2048]{2,1,0:T(8,128)(2,1)S(1)}, bf16[1,512,2048]{2,1,0:T(8,128)(2,1)}, u32[]{:S(2)}) copy-start(bf16[1,512,2048]{2,1,0:T(8,128)(2,1)} %param.12) | copy-start | bytes 6291460
  19.4 14.4 %collective-permute-start.9 = (bf16[128,2048]{1,0:T(8,128)(2,1)S(1)}, bf16[128,2048]{1,0:T(8,128)(2,1)S(1)}, u32[]{:S(2)}, u32[]{:S(2)}) collective-permute-start(bf16[128,2048]{1,0:T(8,128)(2,1)S(1)} %pack.8), channel_id=1, source_target_pairs={{0,8},{1,9},{2,10},{3,11},{4,12},{5,13},{6,14},{7,15},{8,0},{9,1},... | collective-permute-start | bytes 1572872 | tf_op jit(solution)/shard_map/ppermute | solution.py:197
  20.1 12.4 %collective-permute-start.7 = (bf16[96,2048]{1,0:T(8,128)(2,1)S(1)}, bf16[96,2048]{1,0:T(8,128)(2,1)S(1)}, u32[]{:S(2)}, u32[]{:S(2)}) collective-permute-start(bf16[96,2048]{1,0:T(8,128)(2,1)S(1)} %get-tuple-element.55), channel_id=1, source_target_pairs={{0,2},{1,3},{2,4},{3,5},{4,6},{5,7},{6,0},{7,1},{8,10},{9,11},{10,... | collective-permute-start | bytes 1179656 | tf_op jit(solution)/shard_map/ppermute | solution.py:201
  20.4 12.1 %collective-permute-start.8 = (bf16[96,2048]{1,0:T(8,128)(2,1)S(1)}, bf16[96,2048]{1,0:T(8,128)(2,1)S(1)}, u32[]{:S(2)}, u32[]{:S(2)}) collective-permute-start(bf16[96,2048]{1,0:T(8,128)(2,1)S(1)} %get-tuple-element.56), channel_id=1, source_target_pairs={{0,6},{1,7},{2,0},{3,1},{4,2},{5,3},{6,4},{7,5},{8,14},{9,15},{10,... | collective-permute-start | bytes 1179656 | tf_op jit(solution)/shard_map/ppermute | solution.py:205
  34.3 7.6 %collective-permute-start.10 = (bf16[320,2048]{1,0:T(8,128)(2,1)S(1)}, bf16[320,2048]{1,0:T(8,128)(2,1)S(1)}, u32[]{:S(2)}, u32[]{:S(2)}) collective-permute-start(bf16[320,2048]{1,0:T(8,128)(2,1)S(1)} %pack.9.refs_0_.refs_4_), channel_id=1, source_target_pairs={{0,1},{1,0},{2,3},{3,2},{4,5},{5,4},{6,7},{7,6},{8,9},{9,8},{10,11... | collective-permute-start | bytes 3932168 | tf_op jit(solution)/shard_map/ppermute | solution.py:209
  35.5 10.0 %collective-permute-start.11 = (bf16[64,2048]{1,0:T(8,128)(2,1)S(1)}, bf16[64,2048]{1,0:T(8,128)(2,1)S(1)}, u32[]{:S(2)}, u32[]{:S(2)}) collective-permute-start(bf16[64,2048]{1,0:T(8,128)(2,1)S(1)} %get-tuple-element.58), channel_id=1, source_target_pairs={{0,2},{1,3},{2,4},{3,5},{4,6},{5,7},{6,0},{7,1},{8,10},{9,11},{10,... | collective-permute-start | bytes 786440 | tf_op jit(solution)/shard_map/ppermute | solution.py:201
  35.6 9.9 %collective-permute-start.12 = (bf16[64,2048]{1,0:T(8,128)(2,1)S(1)}, bf16[64,2048]{1,0:T(8,128)(2,1)S(1)}, u32[]{:S(2)}, u32[]{:S(2)}) collective-permute-start(bf16[64,2048]{1,0:T(8,128)(2,1)S(1)} %get-tuple-element.59), channel_id=1, source_target_pairs={{0,6},{1,7},{2,0},{3,1},{4,2},{5,3},{6,4},{7,5},{8,14},{9,15},{10,... | collective-permute-start | bytes 786440 | tf_op jit(solution)/shard_map/ppermute | solution.py:205
  38.8 8.1 %collective-permute-start.13 = (bf16[64,2048]{1,0:T(8,128)(2,1)S(1)}, bf16[64,2048]{1,0:T(8,128)(2,1)S(1)}, u32[]{:S(2)}, u32[]{:S(2)}) collective-permute-start(bf16[64,2048]{1,0:T(8,128)(2,1)S(1)} %get-tuple-element.60), channel_id=1, source_target_pairs={{0,8},{1,9},{2,10},{3,11},{4,12},{5,13},{6,14},{7,15},{8,0},{9,1},... | collective-permute-start | bytes 786440 | tf_op jit(solution)/shard_map/ppermute | solution.py:197
  47.0 27.5 %copy-start.4 = (f32[512]{0:T(512)S(1)}, f32[512]{0:T(512)}, u32[]{:S(2)}) copy-start(f32[512]{0:T(512)} %param.13) | copy-start | bytes 6148
  47.0 2.4 %collective-permute-start.14 = (bf16[192,2048]{1,0:T(8,128)(2,1)S(1)}, bf16[192,2048]{1,0:T(8,128)(2,1)S(1)}, u32[]{:S(2)}, u32[]{:S(2)}) collective-permute-start(bf16[192,2048]{1,0:T(8,128)(2,1)S(1)} %pack.11.refs_2_.refs_6_), channel_id=1, source_target_pairs={{0,1},{1,0},{2,3},{3,2},{4,5},{5,4},{6,7},{7,6},{8,9},{9,8},{10,11... | collective-permute-start | bytes 2359304 | tf_op jit(solution)/shard_map/ppermute | solution.py:209

commit v4 on v3

--- a/solution.py
+++ b/solution.py
@@ -130,45 +130,43 @@
     sums_ref, rank_ref = refs[:2]
     pieces = refs[2:-8]
     enc_ref, dec_ref, bias_ref, code_ref, pre_ref, enc_tile, dec_tile, sems = refs[-8:]
-    total = jnp.zeros(bias_ref.shape, jnp.float32)
+    blocks = []
     chunk = token = 0
     for size in sizes:
         for block in range(size // 64):
-            rank = rank_ref[token : token + 64, :]
             at = slice(block % 2 * 32, (block % 2 + 1) * 32)
-            code = sums_ref[chunk + block // 2, at, :].astype(jnp.float32)
-            code_ref[token : token + 64, :] = spread(code, rank).astype(code_ref.dtype)
-            pre = sums_ref[chunk + size // 128 + block // 2, at, :].astype(jnp.float32)
-            pre = spread(pre, rank)
+            blocks.append((token, chunk + block // 2, chunk + size // 128 + block // 2, at))
+            token += 64
+        chunk += size // 64
+    for token, chunk, _, at in blocks:
+        code = spread(sums_ref[chunk, at, :].astype(jnp.float32), rank_ref[token : token + 64, :])
+        code_ref[token : token + 64, :] = code.astype(code_ref.dtype)
+
+    steps, cut = enc_tile.shape[:2]
+    over_tokens = (((0,), (0,)), ((), ()))
+    columns = [slice(step * cut, (step + 1) * cut) for step in range(steps)]
+    copies = []
+    total = jnp.zeros(bias_ref.shape, jnp.float32)
+    for step in range(steps):
+        dec = lax.dot_general(
+            code_ref[...], read(pieces, cots_at, columns[step]), over_tokens, preferred_element_type=jnp.float32
+        )
+        dec_tile[step] = dec.astype(dec_tile.dtype)
+        copies.append(pltpu.make_async_copy(dec_tile.at[step], dec_ref.at[:, columns[step]], sems.at[0, step]))
+        copies[-1].start()
+        for token, _, chunk, at in blocks[step * len(blocks) // steps : (step + 1) * len(blocks) // steps]:
+            pre = spread(sums_ref[chunk, at, :].astype(jnp.float32), rank_ref[token : token + 64, :])
             pre_ref[token : token + 64, :] = pre.astype(pre_ref.dtype)
             total += jnp.sum(pre, axis=0, keepdims=True)
-            token += 64
-        chunk += size // 64
     bias_ref[...] = total
-
-    cut = enc_tile.shape[1]
-    over_tokens = (((0,), (0,)), ((), ()))
-    out = [[], []]
-    for step in range(enc_ref.shape[0] // cut):
-        columns = slice(step * cut, (step + 1) * cut)
-        side = step % 2
-        for copy in out[side]:
-            copy.wait()
-        dec = lax.dot_general(
-            code_ref[...], read(pieces, cots_at, columns), over_tokens, preferred_element_type=jnp.float32
+    for step in range(steps):
+        enc = lax.dot_general(
+            read(pieces, acts_at, columns[step]), pre_ref[...], over_tokens, preferred_element_type=jnp.float32
         )
-        dec_tile[side] = dec.astype(dec_tile.dtype)
-        enc = lax.dot_general(
-            read(pieces, acts_at, columns), pre_ref[...], over_tokens, preferred_element_type=jnp.float32
-        )
-        enc_tile[side] = enc.astype(enc_tile.dtype)
-        out[side] = [
-            pltpu.make_async_copy(dec_tile.at[side], dec_ref.at[:, columns], sems.at[0, side]),
-            pltpu.make_async_copy(enc_tile.at[side], enc_ref.at[columns, :], sems.at[1, side]),
-        ]
-        for copy in out[side]:
-            copy.start()
-    for copy in out[0] + out[1]:
+        enc_tile[step] = enc.astype(enc_tile.dtype)
+        copies.append(pltpu.make_async_copy(enc_tile.at[step], enc_ref.at[columns[step], :], sems.at[1, step]))
+        copies[-1].start()
+    for copy in copies:
         copy.wait()
 
 
@@ -378,11 +376,11 @@
         scratch_shapes=[
             pltpu.VMEM((tokens, latents), bf16),
             pltpu.VMEM((tokens, latents), bf16),
-            pltpu.VMEM((2, cut, latents), bf16),
-            pltpu.VMEM((2, latents, cut), bf16),
-            pltpu.SemaphoreType.DMA((2, 2)),
+            pltpu.VMEM((width // cut, cut, latents), bf16),
+            pltpu.VMEM((width // cut, latents, cut), bf16),
+            pltpu.SemaphoreType.DMA((2, width // cut)),
         ],
-        compiler_params=params(16),
+        compiler_params=params(20),
         name="grads",
     )(sums, rank, *doubled)
     return enc_grad[None], dec_grad[None], bias_grad[0]

time: 101 us -> 100 us (0.990)
  no operation moved by 1% of the time
where the time goes in v4:
time: 100 us
  blocking collectives  39.6 us (40%)
  Pallas kernels  21 us (21%)
  waiting for transfers between devices  20.8 us (21%)
  starting transfers between devices  15.4 us (15%)
  local copies, waits for them, and re-layouts  1.62 us (2%)
  between operations  1.03 us (1%)
    all_to_all x1, blocking collectives, local(): mine = lax.all_to_all(terms, 'layer', 0, 0)  23.7 us
    all_to_all x1, blocking collectives, local(): sums = lax.all_to_all(sums, 'layer', 0, 0)  15.9 us
    ppermute x4, waiting for transfers between devices, up(): return lax.ppermute(values, 'latent', hop(0, 1, 0))  12.3 us
    ppermute x4, starting transfers between devices, down(): return lax.ppermute(values, 'latent', hop(0, -1, 0))  11.7 us
    pallas_call x1, Pallas kernels, local(): pl.pallas_call(functools.partial(grad_kernel, all_acts, all_cots, sizes),...  8.99 us
    ppermute x4, waiting for transfers between devices, east(): return lax.ppermute(values, 'latent', hop(1, 0, 0))  6.17 us
    pallas_call x3, Pallas kernels, terms_of(): pl.pallas_call(functools.partial(term_kernel, *at, start, len(earlier)),...  5.28 us
    pallas_call x1, Pallas kernels, local(): pl.pallas_call(rank_kernel, in_specs=[smem, whole()], out_specs=[whole(),...  3.73 us
  transfers between devices with their start and end apart: 15, of which 7 were waited for; matrix products, arithmetic and copies ran while one was open for 1% of the time, Pallas kernels for 10%

profile of v4, /device:TPU:2, one launch (start us, length us, event | category | flops | bytes accessed | tf_op | source)
XLA Modules:
  0.0 100.3 jit_solution(8014042362226594948)
XLA Ops:
  0.6 3.1 %collective-permute-start.4 = (bf16[64,2048]{1,0:T(8,128)(2,1)}, bf16[64,2048]{1,0:T(8,128)(2,1)S(1)}, u32[]{:S(2)}, u32[]{:S(2)}) collective-permute-start(bf16[64,2048]{1,0:T(8,128)(2,1)} %bitcast.16), channel_id=1, source_target_pairs={{0,6},{1,7},{2,0},{3,1},{4,2},{5,3},{6,4},{7,5},{8,14},{9,15},{10,... | collective-permute-start | bytes 786440 | tf_op jit(solution)/shard_map/ppermute | solution.py:203
  3.7 1.3 %collective-permute-start = (bf16[64,2048]{1,0:T(8,128)(2,1)}, bf16[64,2048]{1,0:T(8,128)(2,1)S(1)}, u32[]{:S(2)}, u32[]{:S(2)}) collective-permute-start(bf16[64,2048]{1,0:T(8,128)(2,1)} %bitcast.18), channel_id=1, source_target_pairs={{0,8},{1,9},{2,10},{3,11},{4,12},{5,13},{6,14},{7,15},{8,0},{9,1},... | collective-permute-start | bytes 786440 | tf_op jit(solution)/shard_map/ppermute | solution.py:195
  5.0 2.5 %collective-permute-start.2 = (bf16[64,2048]{1,0:T(8,128)(2,1)}, bf16[64,2048]{1,0:T(8,128)(2,1)S(1)}, u32[]{:S(2)}, u32[]{:S(2)}) collective-permute-start(bf16[64,2048]{1,0:T(8,128)(2,1)} %bitcast.20), channel_id=1, source_target_pairs={{0,6},{1,7},{2,0},{3,1},{4,2},{5,3},{6,4},{7,5},{8,14},{9,15},{10,... | collective-permute-start | bytes 786440 | tf_op jit(solution)/shard_map/ppermute | solution.py:203
  7.6 0.7 fusion.1.order_ref
  8.3 3.4 %collective-permute-done.refs_0_.refs_2_ = bf16[64,2048]{1,0:T(8,128)(2,1)S(1)} collective-permute-done((bf16[64,2048]{1,0:T(8,128)(2,1)}, bf16[64,2048]{1,0:T(8,128)(2,1)S(1)}, u32[]{:S(2)}, u32[]{:S(2)}) %collective-permute-start) | collective-permute-done | bytes 262176 | tf_op jit(solution)/shard_map/ppermute | solution.py:195
  12.2 1.6 %copy-done.5 = s32[1024,512]{1,0:T(8,128)S(1)} copy-done((s32[1024,512]{1,0:T(8,128)S(1)}, s32[1024,512]{1,0:T(8,128)}, u32[]{:S(2)}) %copy-start.5) | copy-done | bytes 2097176
  13.8 3.7 %ranks.1 = (s32[1024,512]{1,0:T(8,128)S(1)}, s32[512,128]{1,0:T(8,128)S(1)}) custom-call(s32[16]{0:T(128)S(1)} %fusion.1.order_ref, s32[1024,512]{1,0:T(8,128)S(1)} %copy-done.5), custom_call_target="tpu_custom_call" | custom-call | flops 3000000000 | bytes 4000000 | tf_op jit(solution)/shard_map/ranks/pallas_call | solution.py:282
  17.6 0.9 collective-permute-done.1.refs_1_.refs_3_.refs_0_
  19.4 0.7 collective-permute-start.9
  20.4 2.9 %collective-permute-start.8 = (bf16[96,2048]{1,0:T(8,128)(2,1)S(1)}, bf16[96,2048]{1,0:T(8,128)(2,1)S(1)}, u32[]{:S(2)}, u32[]{:S(2)}) collective-permute-start(bf16[96,2048]{1,0:T(8,128)(2,1)S(1)} %get-tuple-element.56), channel_id=1, source_target_pairs={{0,6},{1,7},{2,0},{3,1},{4,2},{5,3},{6,4},{7,5},{8,14},{9,15},{10,... | collective-permute-start | bytes 1179656 | tf_op jit(solution)/shard_map/ppermute | solution.py:203
  23.3 9.2 %collective-permute-done.7.refs_0_.refs_3_ = bf16[96,2048]{1,0:T(8,128)(2,1)S(1)} collective-permute-done((bf16[96,2048]{1,0:T(8,128)(2,1)S(1)}, bf16[96,2048]{1,0:T(8,128)(2,1)S(1)}, u32[]{:S(2)}, u32[]{:S(2)}) %collective-permute-start.7) | collective-permute-done | bytes 393248 | tf_op jit(solution)/shard_map/ppermute | solution.py:199
  32.5 1.3 %collective-permute-done.9.refs_2_ = bf16[128,2048]{1,0:T(8,128)(2,1)S(1)} collective-permute-done((bf16[128,2048]{1,0:T(8,128)(2,1)S(1)}, bf16[128,2048]{1,0:T(8,128)(2,1)S(1)}, u32[]{:S(2)}, u32[]{:S(2)}) %collective-permute-start.9) | collective-permute-done | bytes 524320 | tf_op jit(solution)/shard_map/ppermute | solution.py:195
  34.4 1.1 %pack.10 = (bf16[64,2048]{1,0:T(8,128)(2,1)S(1)}, bf16[64,2048]{1,0:T(8,128)(2,1)S(1)}, bf16[64,2048]{1,0:T(8,128)(2,1)S(1)}) custom-call(bf16[96,2048]{1,0:T(8,128)(2,1)S(1)} %collective-permute-done.7.refs_0_.refs_3_, bf16[96,2048]{1,0:T(8,128)(2,1)S(1)} %collective-permute-done.8.refs_1_.refs_5_, ...), custom_call_target="tpu_custom_call" | custom-call | bytes 1572864 | tf_op jit(solution)/shard_map/pack/pallas_call | solution.py:244
  35.6 3.2 %collective-permute-start.12 = (bf16[64,2048]{1,0:T(8,128)(2,1)S(1)}, bf16[64,2048]{1,0:T(8,128)(2,1)S(1)}, u32[]{:S(2)}, u32[]{:S(2)}) collective-permute-start(bf16[64,2048]{1,0:T(8,128)(2,1)S(1)} %get-tuple-element.59), channel_id=1, source_target_pairs={{0,6},{1,7},{2,0},{3,1},{4,2},{5,3},{6,4},{7,5},{8,14},{9,15},{10,... | collective-permute-start | bytes 786440 | tf_op jit(solution)/shard_map/ppermute | solution.py:203
  39.4 2.5 %near.1.refs_5_ = bf16[8,64,128]{2,1,0:T(8,128)(2,1)S(1)} custom-call(bf16[512,2048]{1,0:T(8,128)(2,1)S(1)} %pack.7.refs_0_.refs_2_, bf16[512,2048]{1,0:T(8,128)(2,1)S(1)} %collective-permute-done.6.refs_1_.refs_3_, bf16[2048,512]{1,0:T(8,128)(2,1)S(1)} %bitcast.10, bf16[512,2048]{1,0:T(8,128)(2,1)S(1)} %bitcast.13, ...), custom_call_target="tpu_custom_call" | custom-call | flops 2147483648 | bytes 4194304 | tf_op jit(solution)/shard_map/near/pallas_call | solution.py:332
  41.9 1.4 %middle.1.refs_7_ = bf16[12,64,128]{2,1,0:T(8,128)(2,1)S(1)} custom-call(bf16[320,2048]{1,0:T(8,128)(2,1)S(1)} %pack.9.refs_0_.refs_4_, bf16[320,2048]{1,0:T(8,128)(2,1)S(1)} %collective-permute-done.10.refs_1_.refs_5_, bf16[2048,512]{1,0:T(8,128)(2,1)S(1)} %bitcast.11, bf16[512,2048]{1,0:T(8,128)(2,1)S(1)} %bitcast.14, ...), custom_call_target="tpu_custom_call" | custom-call | flops 1073741824 | bytes 2097152 | tf_op jit(solution)/shard_map/middle/pallas_call | solution.py:332
  43.3 2.1 %collective-permute-done.11.refs_0_ = bf16[64,2048]{1,0:T(8,128)(2,1)S(1)} collective-permute-done((bf16[64,2048]{1,0:T(8,128)(2,1)S(1)}, bf16[64,2048]{1,0:T(8,128)(2,1)S(1)}, u32[]{:S(2)}, u32[]{:S(2)}) %collective-permute-start.11) | collective-permute-done | bytes 262176 | tf_op jit(solution)/shard_map/ppermute | solution.py:199
  45.4 1.5 %collective-permute-done.13.refs_2_ = bf16[64,2048]{1,0:T(8,128)(2,1)S(1)} collective-permute-done((bf16[64,2048]{1,0:T(8,128)(2,1)S(1)}, bf16[64,2048]{1,0:T(8,128)(2,1)S(1)}, u32[]{:S(2)}, u32[]{:S(2)}) %collective-permute-start.13) | collective-permute-done | bytes 262176 | tf_op jit(solution)/shard_map/ppermute | solution.py:195
  47.1 2.3 %collective-permute-done.14.refs_3_.refs_7_ = bf16[192,2048]{1,0:T(8,128)(2,1)S(1)} collective-permute-done((bf16[192,2048]{1,0:T(8,128)(2,1)S(1)}, bf16[192,2048]{1,0:T(8,128)(2,1)S(1)}, u32[]{:S(2)}, u32[]{:S(2)}) %collective-permute-start.14) | collective-permute-done | bytes 786464 | tf_op jit(solution)/shard_map/ppermute | solution.py:207
  49.4 1.4 %far.1 = bf16[16,64,128]{2,1,0:T(8,128)(2,1)S(1)} custom-call(bf16[320,2048]{1,0:T(8,128)(2,1)S(1)} %pack.9.refs_0_.refs_4_, bf16[320,2048]{1,0:T(8,128)(2,1)S(1)} %collective-permute-done.10.refs_1_.refs_5_, bf16[192,2048]{1,0:T(8,128)(2,1)S(1)} %pack.11.refs_2_.refs_6_, bf16[192,2048]{1,0:T(8,128)(2,1)S(1)} %collective-permute-done.14.refs_3_.refs_7_, ...), custom_call_target="tpu_custom_call" | custom-call | flops 1073741824 | bytes 2097152 | tf_op jit(solution)/shard_map/far/pallas_call | solution.py:332
  50.8 23.7 %all_to_all.10.terms_ref = bf16[16,64,128]{2,1,0:T(8,128)(2,1)S(1)} all-to-all(bf16[16,64,128]{2,1,0:T(8,128)(2,1)S(1)} %far.1), channel_id=1, replica_groups=mesh['layer'=16,'latent'=16] {'layer'}, dimensions={0} | all-to-all | bytes 524288 | tf_op jit(solution)/shard_map/all_to_all | solution.py:353
  74.5 0.7 sums.1
  75.2 15.9 %all_to_all.11.refs_0_ = bf16[16,64,128]{2,1,0:T(8,128)(2,1)S(1)} all-to-all(bf16[16,64,128]{2,1,0:T(8,128)(2,1)S(1)} %sums.1), channel_id=1, replica_groups=mesh['layer'=16,'latent'=16] {'layer'}, dimensions={0} | all-to-all | bytes 524288 | tf_op jit(solution)/shard_map/all_to_all | solution.py:362
  91.1 9.0 %grads.1 = (bf16[2048,512]{1,0:T(8,128)(2,1)}, bf16[512,2048]{1,0:T(8,128)(2,1)}, f32[1,512]{1,0:T(1,128)}) custom-call(bf16[16,64,128]{2,1,0:T(8,128)(2,1)S(1)} %all_to_all.11.refs_0_, s32[1024,512]{1,0:T(8,128)S(1)} %get-tuple-element.67.refs_1_, bf16[512,2048]{1,0:T(8,128)(2,1)S(1)} %pack.7.refs_0_.refs_2_, ...), custom_call_target="tpu_custom_call" | custom-call | tf_op jit(solution)/shard_map/grads/pallas_call | solution.py:367
  (34 shorter events, 3.1 us)
Async XLA Ops:
  0.6 18.3 %collective-permute-start.4 = (bf16[64,2048]{1,0:T(8,128)(2,1)}, bf16[64,2048]{1,0:T(8,128)(2,1)S(1)}, u32[]{:S(2)}, u32[]{:S(2)}) collective-permute-start(bf16[64,2048]{1,0:T(8,128)(2,1)} %bitcast.16), channel_id=1, source_target_pairs={{0,6},{1,7},{2,0},{3,1},{4,2},{5,3},{6,4},{7,5},{8,14},{9,15},{10,... | collective-permute-start | bytes 786440 | tf_op jit(solution)/shard_map/ppermute | solution.py:203
  3.7 15.2 %collective-permute-start.3 = (bf16[64,2048]{1,0:T(8,128)(2,1)}, bf16[64,2048]{1,0:T(8,128)(2,1)S(1)}, u32[]{:S(2)}, u32[]{:S(2)}) collective-permute-start(bf16[64,2048]{1,0:T(8,128)(2,1)} %bitcast.17), channel_id=1, source_target_pairs={{0,2},{1,3},{2,4},{3,5},{4,6},{5,7},{6,0},{7,1},{8,10},{9,11},{10,... | collective-permute-start | bytes 786440 | tf_op jit(solution)/shard_map/ppermute | solution.py:199
  3.7 8.0 %collective-permute-start = (bf16[64,2048]{1,0:T(8,128)(2,1)}, bf16[64,2048]{1,0:T(8,128)(2,1)S(1)}, u32[]{:S(2)}, u32[]{:S(2)}) collective-permute-start(bf16[64,2048]{1,0:T(8,128)(2,1)} %bitcast.18), channel_id=1, source_target_pairs={{0,8},{1,9},{2,10},{3,11},{4,12},{5,13},{6,14},{7,15},{8,0},{9,1},... | collective-permute-start | bytes 786440 | tf_op jit(solution)/shard_map/ppermute | solution.py:195
  5.0 12.6 %collective-permute-start.2 = (bf16[64,2048]{1,0:T(8,128)(2,1)}, bf16[64,2048]{1,0:T(8,128)(2,1)S(1)}, u32[]{:S(2)}, u32[]{:S(2)}) collective-permute-start(bf16[64,2048]{1,0:T(8,128)(2,1)} %bitcast.20), channel_id=1, source_target_pairs={{0,6},{1,7},{2,0},{3,1},{4,2},{5,3},{6,4},{7,5},{8,14},{9,15},{10,... | collective-permute-start | bytes 786440 | tf_op jit(solution)/shard_map/ppermute | solution.py:203
  7.5 11.0 %collective-permute-start.1 = (bf16[64,2048]{1,0:T(8,128)(2,1)}, bf16[64,2048]{1,0:T(8,128)(2,1)S(1)}, u32[]{:S(2)}, u32[]{:S(2)}) collective-permute-start(bf16[64,2048]{1,0:T(8,128)(2,1)} %bitcast.21), channel_id=1, source_target_pairs={{0,2},{1,3},{2,4},{3,5},{4,6},{5,7},{6,0},{7,1},{8,10},{9,11},{10,... | collective-permute-start | bytes 786440 | tf_op jit(solution)/shard_map/ppermute | solution.py:199
  8.3 10.7 %copy-start.2 = (bf16[1,64,2048]{2,1,0:T(8,128)(2,1)S(1)}, bf16[1,64,2048]{2,1,0:T(8,128)(2,1)}, u32[]{:S(2)}) copy-start(bf16[1,64,2048]{2,1,0:T(8,128)(2,1)} %param.9) | copy-start | bytes 786436
  8.3 10.7 %copy-start.3 = (bf16[1,64,2048]{2,1,0:T(8,128)(2,1)S(1)}, bf16[1,64,2048]{2,1,0:T(8,128)(2,1)}, u32[]{:S(2)}) copy-start(bf16[1,64,2048]{2,1,0:T(8,128)(2,1)} %param.10) | copy-start | bytes 786436
  11.7 7.3 %collective-permute-start.5 = (bf16[64,2048]{1,0:T(8,128)(2,1)}, bf16[64,2048]{1,0:T(8,128)(2,1)S(1)}, u32[]{:S(2)}, u32[]{:S(2)}) collective-permute-start(bf16[64,2048]{1,0:T(8,128)(2,1)} %bitcast.22), channel_id=1, source_target_pairs={{0,8},{1,9},{2,10},{3,11},{4,12},{5,13},{6,14},{7,15},{8,0},{9,1},... | collective-permute-start | bytes 786440 | tf_op jit(solution)/shard_map/ppermute | solution.py:195
  12.2 1.6 %copy-start.5 = (s32[1024,512]{1,0:T(8,128)S(1)}, s32[1024,512]{1,0:T(8,128)}, u32[]{:S(2)}) copy-start(s32[1024,512]{1,0:T(8,128)} %mask_ref.1) | copy-start | bytes 6291460
  19.2 20.1 %collective-permute-start.6 = (bf16[512,2048]{1,0:T(8,128)(2,1)S(1)}, bf16[512,2048]{1,0:T(8,128)(2,1)S(1)}, u32[]{:S(2)}, u32[]{:S(2)}) collective-permute-start(bf16[512,2048]{1,0:T(8,128)(2,1)S(1)} %pack.7.refs_0_.refs_2_), channel_id=1, source_target_pairs={{0,1},{1,0},{2,3},{3,2},{4,5},{5,4},{6,7},{7,6},{8,9},{9,8},{10,11... | collective-permute-start | bytes 6291464 | tf_op jit(solution)/shard_map/ppermute | solution.py:207
  19.4 20.0 %copy-start = (bf16[1,2048,512]{2,1,0:T(8,128)(2,1)S(1)}, bf16[1,2048,512]{2,1,0:T(8,128)(2,1)}, u32[]{:S(2)}) copy-start(bf16[1,2048,512]{2,1,0:T(8,128)(2,1)} %param.11) | copy-start | bytes 6291460
  19.4 19.9 %copy-start.1 = (bf16[1,512,2048]{2,1,0:T(8,128)(2,1)S(1)}, bf16[1,512,2048]{2,1,0:T(8,128)(2,1)}, u32[]{:S(2)}) copy-start(bf16[1,512,2048]{2,1,0:T(8,128)(2,1)} %param.12) | copy-start | bytes 6291460
  19.4 14.4 %collective-permute-start.9 = (bf16[128,2048]{1,0:T(8,128)(2,1)S(1)}, bf16[128,2048]{1,0:T(8,128)(2,1)S(1)}, u32[]{:S(2)}, u32[]{:S(2)}) collective-permute-start(bf16[128,2048]{1,0:T(8,128)(2,1)S(1)} %pack.8), channel_id=1, source_target_pairs={{0,8},{1,9},{2,10},{3,11},{4,12},{5,13},{6,14},{7,15},{8,0},{9,1},... | collective-permute-start | bytes 1572872 | tf_op jit(solution)/shard_map/ppermute | solution.py:195
  20.1 12.4 %collective-permute-start.7 = (bf16[96,2048]{1,0:T(8,128)(2,1)S(1)}, bf16[96,2048]{1,0:T(8,128)(2,1)S(1)}, u32[]{:S(2)}, u32[]{:S(2)}) collective-permute-start(bf16[96,2048]{1,0:T(8,128)(2,1)S(1)} %get-tuple-element.55), channel_id=1, source_target_pairs={{0,2},{1,3},{2,4},{3,5},{4,6},{5,7},{6,0},{7,1},{8,10},{9,11},{10,... | collective-permute-start | bytes 1179656 | tf_op jit(solution)/shard_map/ppermute | solution.py:199
  20.4 12.1 %collective-permute-start.8 = (bf16[96,2048]{1,0:T(8,128)(2,1)S(1)}, bf16[96,2048]{1,0:T(8,128)(2,1)S(1)}, u32[]{:S(2)}, u32[]{:S(2)}) collective-permute-start(bf16[96,2048]{1,0:T(8,128)(2,1)S(1)} %get-tuple-element.56), channel_id=1, source_target_pairs={{0,6},{1,7},{2,0},{3,1},{4,2},{5,3},{6,4},{7,5},{8,14},{9,15},{10,... | collective-permute-start | bytes 1179656 | tf_op jit(solution)/shard_map/ppermute | solution.py:203
  34.3 7.6 %collective-permute-start.10 = (bf16[320,2048]{1,0:T(8,128)(2,1)S(1)}, bf16[320,2048]{1,0:T(8,128)(2,1)S(1)}, u32[]{:S(2)}, u32[]{:S(2)}) collective-permute-start(bf16[320,2048]{1,0:T(8,128)(2,1)S(1)} %pack.9.refs_0_.refs_4_), channel_id=1, source_target_pairs={{0,1},{1,0},{2,3},{3,2},{4,5},{5,4},{6,7},{7,6},{8,9},{9,8},{10,11... | collective-permute-start | bytes 3932168 | tf_op jit(solution)/shard_map/ppermute | solution.py:207
  35.5 10.0 %collective-permute-start.11 = (bf16[64,2048]{1,0:T(8,128)(2,1)S(1)}, bf16[64,2048]{1,0:T(8,128)(2,1)S(1)}, u32[]{:S(2)}, u32[]{:S(2)}) collective-permute-start(bf16[64,2048]{1,0:T(8,128)(2,1)S(1)} %get-tuple-element.58), channel_id=1, source_target_pairs={{0,2},{1,3},{2,4},{3,5},{4,6},{5,7},{6,0},{7,1},{8,10},{9,11},{10,... | collective-permute-start | bytes 786440 | tf_op jit(solution)/shard_map/ppermute | solution.py:199
  35.6 9.9 %collective-permute-start.12 = (bf16[64,2048]{1,0:T(8,128)(2,1)S(1)}, bf16[64,2048]{1,0:T(8,128)(2,1)S(1)}, u32[]{:S(2)}, u32[]{:S(2)}) collective-permute-start(bf16[64,2048]{1,0:T(8,128)(2,1)S(1)} %get-tuple-element.59), channel_id=1, source_target_pairs={{0,6},{1,7},{2,0},{3,1},{4,2},{5,3},{6,4},{7,5},{8,14},{9,15},{10,... | collective-permute-start | bytes 786440 | tf_op jit(solution)/shard_map/ppermute | solution.py:203
  38.8 8.1 %collective-permute-start.13 = (bf16[64,2048]{1,0:T(8,128)(2,1)S(1)}, bf16[64,2048]{1,0:T(8,128)(2,1)S(1)}, u32[]{:S(2)}, u32[]{:S(2)}) collective-permute-start(bf16[64,2048]{1,0:T(8,128)(2,1)S(1)} %get-tuple-element.60), channel_id=1, source_target_pairs={{0,8},{1,9},{2,10},{3,11},{4,12},{5,13},{6,14},{7,15},{8,0},{9,1},... | collective-permute-start | bytes 786440 | tf_op jit(solution)/shard_map/ppermute | solution.py:195
  47.0 27.5 %copy-start.4 = (f32[512]{0:T(512)S(1)}, f32[512]{0:T(512)}, u32[]{:S(2)}) copy-start(f32[512]{0:T(512)} %param.13) | copy-start | bytes 6148
  47.0 2.4 %collective-permute-start.14 = (bf16[192,2048]{1,0:T(8,128)(2,1)S(1)}, bf16[192,2048]{1,0:T(8,128)(2,1)S(1)}, u32[]{:S(2)}, u32[]{:S(2)}) collective-permute-start(bf16[192,2048]{1,0:T(8,128)(2,1)S(1)} %pack.11.refs_2_.refs_6_), channel_id=1, source_target_pairs={{0,1},{1,0},{2,3},{3,2},{4,5},{5,4},{6,7},{7,6},{8,9},{9,8},{10,11... | collective-permute-start | bytes 2359304 | tf_op jit(solution)/shard_map/ppermute | solution.py:207

commit v5 on v4

--- a/solution.py
+++ b/solution.py
@@ -314,12 +314,12 @@
     acts_at = [
         [[(0, k * rows, (k + 1) * rows)] for k in (0, 2, 5, 6)],
         [[(1, 0, 64)], [(1, 96, 160)]],
-        [[(2, 0, 32), (2, 64, 96)], [(2, 32, 64), (2, 96, 128)]],
+        [[(2, 0, 32), (3, 0, 32)], [(2, 32, 64), (3, 32, 64)]],
     ]
     cots_at = [
         [[(0, k * rows, (k + 1) * rows)] for k in (1, 7, 3, 4)],
         [[(1, 192, 256)], [(1, 256, 320)]],
-        [[(1, 64, 96), (1, 160, 192)], [(2, 128, 192)]],
+        [[(1, 64, 96), (1, 160, 192)], [(2, 64, 128)]],
     ]
 
     def with_twins(items, first=0):
@@ -345,9 +345,9 @@
     terms = terms_of(0, [], doubled)
     doubled += [second, twin(second)]
     terms = terms_of(1, [terms], doubled[2:])
-    *doubled, terms, fourth_low, fourth_high, c_x_far = tie((*doubled, terms, fourth_low, fourth_high, c_x_far))
-    last = pack(fourth_low, fourth_high, c_x_far)
-    doubled += [last, twin(last)]
+    *doubled, terms, fourth_low, c_x_far = tie((*doubled, terms, fourth_low, c_x_far))
+    last = pack(fourth_low, c_x_far)
+    doubled += [last, twin(last), fourth_high, twin(fourth_high)]
     terms = terms_of(2, [terms], doubled[2:])
 
     mine = lax.all_to_all(terms, "layer", 0, 0)

time: 100 us -> 99.8 us (level); the launches traced: 100 us -> 98.8 us
  waiting for transfers between devices: 20.8 us -> 18.8 us
    ppermute x4, waiting for transfers between devices: 6.17 us -> 4.71 us  [east(): return lax.ppermute(values, 'latent', hop(1, 0, 0))]
    ppermute x3 -> x4, waiting for transfers between devices: 2.28 us -> 1.78 us  [twin(): return lax.ppermute(values, 'latent', hop(0, 0, 1))]
  transfers between devices with their start and end apart: 15 -> 16, of which waited for: 7 -> 6; matrix products, arithmetic and copies ran while one was open for 1% -> 1% of each run, Pallas kernels for 10% -> 10%
where the time goes in v5:
time: 99.8 us; the launch traced here: 98.8 us
  blocking collectives  39.6 us (40%)
  Pallas kernels  21 us (21%)
  waiting for transfers between devices  18.8 us (19%)
  starting transfers between devices  15.9 us (16%)
  local copies, waits for them, and re-layouts  1.62 us (2%)
  between operations  1.04 us (1%)
    all_to_all x1, blocking collectives, local(): mine = lax.all_to_all(terms, 'layer', 0, 0)  23.7 us
    all_to_all x1, blocking collectives, local(): sums = lax.all_to_all(sums, 'layer', 0, 0)  15.9 us
    ppermute x4, waiting for transfers between devices, up(): return lax.ppermute(values, 'latent', hop(0, 1, 0))  12.3 us
    ppermute x4, starting transfers between devices, down(): return lax.ppermute(values, 'latent', hop(0, -1, 0))  11.4 us
    pallas_call x1, Pallas kernels, local(): pl.pallas_call(functools.partial(grad_kernel, all_acts, all_cots, sizes),...  8.98 us
    pallas_call x3, Pallas kernels, terms_of(): pl.pallas_call(functools.partial(term_kernel, *at, start, len(earlier)),...  5.28 us
    ppermute x4, waiting for transfers between devices, east(): return lax.ppermute(values, 'latent', hop(1, 0, 0))  4.71 us
    pallas_call x1, Pallas kernels, local(): pl.pallas_call(rank_kernel, in_specs=[smem, whole()], out_specs=[whole(),...  3.73 us
  transfers between devices with their start and end apart: 16, of which 6 were waited for; matrix products, arithmetic and copies ran while one was open for 1% of the time, Pallas kernels for 10%

profile of v5, /device:TPU:2, one launch (start us, length us, event | category | flops | bytes accessed | tf_op | source)
XLA Modules:
  0.0 98.8 jit_solution(559137210853195839)
XLA Ops:
  0.6 3.1 %collective-permute-start.4 = (bf16[64,2048]{1,0:T(8,128)(2,1)}, bf16[64,2048]{1,0:T(8,128)(2,1)S(1)}, u32[]{:S(2)}, u32[]{:S(2)}) collective-permute-start(bf16[64,2048]{1,0:T(8,128)(2,1)} %bitcast.16), channel_id=1, source_target_pairs={{0,6},{1,7},{2,0},{3,1},{4,2},{5,3},{6,4},{7,5},{8,14},{9,15},{10,... | collective-permute-start | bytes 786440 | tf_op jit(solution)/shard_map/ppermute | solution.py:203
  3.7 1.3 %collective-permute-start = (bf16[64,2048]{1,0:T(8,128)(2,1)}, bf16[64,2048]{1,0:T(8,128)(2,1)S(1)}, u32[]{:S(2)}, u32[]{:S(2)}) collective-permute-start(bf16[64,2048]{1,0:T(8,128)(2,1)} %bitcast.18), channel_id=1, source_target_pairs={{0,8},{1,9},{2,10},{3,11},{4,12},{5,13},{6,14},{7,15},{8,0},{9,1},... | collective-permute-start | bytes 786440 | tf_op jit(solution)/shard_map/ppermute | solution.py:195
  5.0 2.5 %collective-permute-start.2 = (bf16[64,2048]{1,0:T(8,128)(2,1)}, bf16[64,2048]{1,0:T(8,128)(2,1)S(1)}, u32[]{:S(2)}, u32[]{:S(2)}) collective-permute-start(bf16[64,2048]{1,0:T(8,128)(2,1)} %bitcast.20), channel_id=1, source_target_pairs={{0,6},{1,7},{2,0},{3,1},{4,2},{5,3},{6,4},{7,5},{8,14},{9,15},{10,... | collective-permute-start | bytes 786440 | tf_op jit(solution)/shard_map/ppermute | solution.py:203
  7.6 0.7 fusion.1.order_ref
  8.3 3.4 %collective-permute-done.refs_0_.refs_2_ = bf16[64,2048]{1,0:T(8,128)(2,1)S(1)} collective-permute-done((bf16[64,2048]{1,0:T(8,128)(2,1)}, bf16[64,2048]{1,0:T(8,128)(2,1)S(1)}, u32[]{:S(2)}, u32[]{:S(2)}) %collective-permute-start) | collective-permute-done | bytes 262176 | tf_op jit(solution)/shard_map/ppermute | solution.py:195
  12.2 1.6 %copy-done.5 = s32[1024,512]{1,0:T(8,128)S(1)} copy-done((s32[1024,512]{1,0:T(8,128)S(1)}, s32[1024,512]{1,0:T(8,128)}, u32[]{:S(2)}) %copy-start.5) | copy-done | bytes 2097176
  13.8 3.7 %ranks.1 = (s32[1024,512]{1,0:T(8,128)S(1)}, s32[512,128]{1,0:T(8,128)S(1)}) custom-call(s32[16]{0:T(128)S(1)} %fusion.1.order_ref, s32[1024,512]{1,0:T(8,128)S(1)} %copy-done.5), custom_call_target="tpu_custom_call" | custom-call | flops 3000000000 | bytes 4000000 | tf_op jit(solution)/shard_map/ranks/pallas_call | solution.py:282
  17.6 0.9 collective-permute-done.1.refs_1_.refs_3_.refs_0_
  19.4 0.7 collective-permute-start.9
  20.4 2.9 %collective-permute-start.8 = (bf16[96,2048]{1,0:T(8,128)(2,1)S(1)}, bf16[96,2048]{1,0:T(8,128)(2,1)S(1)}, u32[]{:S(2)}, u32[]{:S(2)}) collective-permute-start(bf16[96,2048]{1,0:T(8,128)(2,1)S(1)} %get-tuple-element.55), channel_id=1, source_target_pairs={{0,6},{1,7},{2,0},{3,1},{4,2},{5,3},{6,4},{7,5},{8,14},{9,15},{10,... | collective-permute-start | bytes 1179656 | tf_op jit(solution)/shard_map/ppermute | solution.py:203
  23.3 9.2 %collective-permute-done.7.refs_0_.refs_3_ = bf16[96,2048]{1,0:T(8,128)(2,1)S(1)} collective-permute-done((bf16[96,2048]{1,0:T(8,128)(2,1)S(1)}, bf16[96,2048]{1,0:T(8,128)(2,1)S(1)}, u32[]{:S(2)}, u32[]{:S(2)}) %collective-permute-start.7) | collective-permute-done | bytes 393248 | tf_op jit(solution)/shard_map/ppermute | solution.py:199
  32.5 1.3 %collective-permute-done.9.refs_2_ = bf16[128,2048]{1,0:T(8,128)(2,1)S(1)} collective-permute-done((bf16[128,2048]{1,0:T(8,128)(2,1)S(1)}, bf16[128,2048]{1,0:T(8,128)(2,1)S(1)}, u32[]{:S(2)}, u32[]{:S(2)}) %collective-permute-start.9) | collective-permute-done | bytes 524320 | tf_op jit(solution)/shard_map/ppermute | solution.py:195
  34.4 1.1 %pack.10 = (bf16[64,2048]{1,0:T(8,128)(2,1)S(1)}, bf16[64,2048]{1,0:T(8,128)(2,1)S(1)}, bf16[64,2048]{1,0:T(8,128)(2,1)S(1)}) custom-call(bf16[96,2048]{1,0:T(8,128)(2,1)S(1)} %collective-permute-done.7.refs_0_.refs_3_, bf16[96,2048]{1,0:T(8,128)(2,1)S(1)} %collective-permute-done.8.refs_1_.refs_5_, ...), custom_call_target="tpu_custom_call" | custom-call | bytes 1572864 | tf_op jit(solution)/shard_map/pack/pallas_call | solution.py:244
  35.6 0.9 collective-permute-start.12
  36.4 2.9 %collective-permute-start.14 = (bf16[64,2048]{1,0:T(8,128)(2,1)S(1)}, bf16[64,2048]{1,0:T(8,128)(2,1)S(1)}, u32[]{:S(2)}, u32[]{:S(2)}) collective-permute-start(bf16[64,2048]{1,0:T(8,128)(2,1)S(1)} %get-tuple-element.63), channel_id=1, source_target_pairs={{0,6},{1,7},{2,0},{3,1},{4,2},{5,3},{6,4},{7,5},{8,14},{9,15},{10,... | collective-permute-start | bytes 786440 | tf_op jit(solution)/shard_map/ppermute | solution.py:203
  39.4 2.5 %near.1.refs_5_ = bf16[8,64,128]{2,1,0:T(8,128)(2,1)S(1)} custom-call(bf16[512,2048]{1,0:T(8,128)(2,1)S(1)} %pack.7.refs_0_.refs_2_, bf16[512,2048]{1,0:T(8,128)(2,1)S(1)} %collective-permute-done.6.refs_1_.refs_3_, bf16[2048,512]{1,0:T(8,128)(2,1)S(1)} %bitcast.10, bf16[512,2048]{1,0:T(8,128)(2,1)S(1)} %bitcast.13, ...), custom_call_target="tpu_custom_call" | custom-call | flops 2147483648 | bytes 4194304 | tf_op jit(solution)/shard_map/near/pallas_call | solution.py:332
  41.9 1.4 %middle.1.refs_9_ = bf16[12,64,128]{2,1,0:T(8,128)(2,1)S(1)} custom-call(bf16[320,2048]{1,0:T(8,128)(2,1)S(1)} %pack.9.refs_0_.refs_4_, bf16[320,2048]{1,0:T(8,128)(2,1)S(1)} %collective-permute-done.10.refs_1_.refs_5_, bf16[2048,512]{1,0:T(8,128)(2,1)S(1)} %bitcast.11, bf16[512,2048]{1,0:T(8,128)(2,1)S(1)} %bitcast.14, ...), custom_call_target="tpu_custom_call" | custom-call | flops 1073741824 | bytes 2097152 | tf_op jit(solution)/shard_map/middle/pallas_call | solution.py:332
  43.3 2.1 %collective-permute-done.11.refs_0_ = bf16[64,2048]{1,0:T(8,128)(2,1)S(1)} collective-permute-done((bf16[64,2048]{1,0:T(8,128)(2,1)S(1)}, bf16[64,2048]{1,0:T(8,128)(2,1)S(1)}, u32[]{:S(2)}, u32[]{:S(2)}) %collective-permute-start.11) | collective-permute-done | bytes 262176 | tf_op jit(solution)/shard_map/ppermute | solution.py:199
  46.1 1.8 %collective-permute-done.15.refs_5_.refs_9_ = bf16[64,2048]{1,0:T(8,128)(2,1)S(1)} collective-permute-done((bf16[64,2048]{1,0:T(8,128)(2,1)S(1)}, bf16[64,2048]{1,0:T(8,128)(2,1)S(1)}, u32[]{:S(2)}, u32[]{:S(2)}) %collective-permute-start.15) | collective-permute-done | bytes 262176 | tf_op jit(solution)/shard_map/ppermute | solution.py:207
  47.9 1.4 %far.1 = bf16[16,64,128]{2,1,0:T(8,128)(2,1)S(1)} custom-call(bf16[320,2048]{1,0:T(8,128)(2,1)S(1)} %pack.9.refs_0_.refs_4_, bf16[320,2048]{1,0:T(8,128)(2,1)S(1)} %collective-permute-done.10.refs_1_.refs_5_, bf16[128,2048]{1,0:T(8,128)(2,1)S(1)} %pack.11.refs_2_.refs_6_, bf16[128,2048]{1,0:T(8,128)(2,1)S(1)} %collective-permute-done.13.refs_3_.refs_7_, ...), custom_call_target="tpu_custom_call" | custom-call | flops 1073741824 | bytes 2097152 | tf_op jit(solution)/shard_map/far/pallas_call | solution.py:332
  49.3 23.7 %all_to_all.10.terms_ref = bf16[16,64,128]{2,1,0:T(8,128)(2,1)S(1)} all-to-all(bf16[16,64,128]{2,1,0:T(8,128)(2,1)S(1)} %far.1), channel_id=1, replica_groups=mesh['layer'=16,'latent'=16] {'layer'}, dimensions={0} | all-to-all | bytes 524288 | tf_op jit(solution)/shard_map/all_to_all | solution.py:353
  73.0 0.7 sums.1
  73.7 15.9 %all_to_all.11.refs_0_ = bf16[16,64,128]{2,1,0:T(8,128)(2,1)S(1)} all-to-all(bf16[16,64,128]{2,1,0:T(8,128)(2,1)S(1)} %sums.1), channel_id=1, replica_groups=mesh['layer'=16,'latent'=16] {'layer'}, dimensions={0} | all-to-all | bytes 524288 | tf_op jit(solution)/shard_map/all_to_all | solution.py:362
  89.6 9.0 %grads.1 = (bf16[2048,512]{1,0:T(8,128)(2,1)}, bf16[512,2048]{1,0:T(8,128)(2,1)}, f32[1,512]{1,0:T(1,128)}) custom-call(bf16[16,64,128]{2,1,0:T(8,128)(2,1)S(1)} %all_to_all.11.refs_0_, s32[1024,512]{1,0:T(8,128)S(1)} %get-tuple-element.65.refs_1_, bf16[512,2048]{1,0:T(8,128)(2,1)S(1)} %pack.7.refs_0_.refs_2_, ...), custom_call_target="tpu_custom_call" | custom-call | tf_op jit(solution)/shard_map/grads/pallas_call | solution.py:367
  (36 shorter events, 3.0 us)
Async XLA Ops:
  0.6 18.3 %collective-permute-start.4 = (bf16[64,2048]{1,0:T(8,128)(2,1)}, bf16[64,2048]{1,0:T(8,128)(2,1)S(1)}, u32[]{:S(2)}, u32[]{:S(2)}) collective-permute-start(bf16[64,2048]{1,0:T(8,128)(2,1)} %bitcast.16), channel_id=1, source_target_pairs={{0,6},{1,7},{2,0},{3,1},{4,2},{5,3},{6,4},{7,5},{8,14},{9,15},{10,... | collective-permute-start | bytes 786440 | tf_op jit(solution)/shard_map/ppermute | solution.py:203
  3.7 15.2 %collective-permute-start.3 = (bf16[64,2048]{1,0:T(8,128)(2,1)}, bf16[64,2048]{1,0:T(8,128)(2,1)S(1)}, u32[]{:S(2)}, u32[]{:S(2)}) collective-permute-start(bf16[64,2048]{1,0:T(8,128)(2,1)} %bitcast.17), channel_id=1, source_target_pairs={{0,2},{1,3},{2,4},{3,5},{4,6},{5,7},{6,0},{7,1},{8,10},{9,11},{10,... | collective-permute-start | bytes 786440 | tf_op jit(solution)/shard_map/ppermute | solution.py:199
  3.7 8.0 %collective-permute-start = (bf16[64,2048]{1,0:T(8,128)(2,1)}, bf16[64,2048]{1,0:T(8,128)(2,1)S(1)}, u32[]{:S(2)}, u32[]{:S(2)}) collective-permute-start(bf16[64,2048]{1,0:T(8,128)(2,1)} %bitcast.18), channel_id=1, source_target_pairs={{0,8},{1,9},{2,10},{3,11},{4,12},{5,13},{6,14},{7,15},{8,0},{9,1},... | collective-permute-start | bytes 786440 | tf_op jit(solution)/shard_map/ppermute | solution.py:195
  5.0 12.6 %collective-permute-start.2 = (bf16[64,2048]{1,0:T(8,128)(2,1)}, bf16[64,2048]{1,0:T(8,128)(2,1)S(1)}, u32[]{:S(2)}, u32[]{:S(2)}) collective-permute-start(bf16[64,2048]{1,0:T(8,128)(2,1)} %bitcast.20), channel_id=1, source_target_pairs={{0,6},{1,7},{2,0},{3,1},{4,2},{5,3},{6,4},{7,5},{8,14},{9,15},{10,... | collective-permute-start | bytes 786440 | tf_op jit(solution)/shard_map/ppermute | solution.py:203
  7.5 11.0 %collective-permute-start.1 = (bf16[64,2048]{1,0:T(8,128)(2,1)}, bf16[64,2048]{1,0:T(8,128)(2,1)S(1)}, u32[]{:S(2)}, u32[]{:S(2)}) collective-permute-start(bf16[64,2048]{1,0:T(8,128)(2,1)} %bitcast.21), channel_id=1, source_target_pairs={{0,2},{1,3},{2,4},{3,5},{4,6},{5,7},{6,0},{7,1},{8,10},{9,11},{10,... | collective-permute-start | bytes 786440 | tf_op jit(solution)/shard_map/ppermute | solution.py:199
  8.3 10.7 %copy-start.2 = (bf16[1,64,2048]{2,1,0:T(8,128)(2,1)S(1)}, bf16[1,64,2048]{2,1,0:T(8,128)(2,1)}, u32[]{:S(2)}) copy-start(bf16[1,64,2048]{2,1,0:T(8,128)(2,1)} %param.9) | copy-start | bytes 786436
  8.3 10.7 %copy-start.3 = (bf16[1,64,2048]{2,1,0:T(8,128)(2,1)S(1)}, bf16[1,64,2048]{2,1,0:T(8,128)(2,1)}, u32[]{:S(2)}) copy-start(bf16[1,64,2048]{2,1,0:T(8,128)(2,1)} %param.10) | copy-start | bytes 786436
  11.7 7.3 %collective-permute-start.5 = (bf16[64,2048]{1,0:T(8,128)(2,1)}, bf16[64,2048]{1,0:T(8,128)(2,1)S(1)}, u32[]{:S(2)}, u32[]{:S(2)}) collective-permute-start(bf16[64,2048]{1,0:T(8,128)(2,1)} %bitcast.22), channel_id=1, source_target_pairs={{0,8},{1,9},{2,10},{3,11},{4,12},{5,13},{6,14},{7,15},{8,0},{9,1},... | collective-permute-start | bytes 786440 | tf_op jit(solution)/shard_map/ppermute | solution.py:195
  12.2 1.6 %copy-start.5 = (s32[1024,512]{1,0:T(8,128)S(1)}, s32[1024,512]{1,0:T(8,128)}, u32[]{:S(2)}) copy-start(s32[1024,512]{1,0:T(8,128)} %mask_ref.1) | copy-start | bytes 6291460
  19.2 20.1 %collective-permute-start.6 = (bf16[512,2048]{1,0:T(8,128)(2,1)S(1)}, bf16[512,2048]{1,0:T(8,128)(2,1)S(1)}, u32[]{:S(2)}, u32[]{:S(2)}) collective-permute-start(bf16[512,2048]{1,0:T(8,128)(2,1)S(1)} %pack.7.refs_0_.refs_2_), channel_id=1, source_target_pairs={{0,1},{1,0},{2,3},{3,2},{4,5},{5,4},{6,7},{7,6},{8,9},{9,8},{10,11... | collective-permute-start | bytes 6291464 | tf_op jit(solution)/shard_map/ppermute | solution.py:207
  19.4 20.0 %copy-start = (bf16[1,2048,512]{2,1,0:T(8,128)(2,1)S(1)}, bf16[1,2048,512]{2,1,0:T(8,128)(2,1)}, u32[]{:S(2)}) copy-start(bf16[1,2048,512]{2,1,0:T(8,128)(2,1)} %param.11) | copy-start | bytes 6291460
  19.4 19.9 %copy-start.1 = (bf16[1,512,2048]{2,1,0:T(8,128)(2,1)S(1)}, bf16[1,512,2048]{2,1,0:T(8,128)(2,1)}, u32[]{:S(2)}) copy-start(bf16[1,512,2048]{2,1,0:T(8,128)(2,1)} %param.12) | copy-start | bytes 6291460
  19.4 14.4 %collective-permute-start.9 = (bf16[128,2048]{1,0:T(8,128)(2,1)S(1)}, bf16[128,2048]{1,0:T(8,128)(2,1)S(1)}, u32[]{:S(2)}, u32[]{:S(2)}) collective-permute-start(bf16[128,2048]{1,0:T(8,128)(2,1)S(1)} %pack.8), channel_id=1, source_target_pairs={{0,8},{1,9},{2,10},{3,11},{4,12},{5,13},{6,14},{7,15},{8,0},{9,1},... | collective-permute-start | bytes 1572872 | tf_op jit(solution)/shard_map/ppermute | solution.py:195
  20.1 12.4 %collective-permute-start.7 = (bf16[96,2048]{1,0:T(8,128)(2,1)S(1)}, bf16[96,2048]{1,0:T(8,128)(2,1)S(1)}, u32[]{:S(2)}, u32[]{:S(2)}) collective-permute-start(bf16[96,2048]{1,0:T(8,128)(2,1)S(1)} %get-tuple-element.54), channel_id=1, source_target_pairs={{0,2},{1,3},{2,4},{3,5},{4,6},{5,7},{6,0},{7,1},{8,10},{9,11},{10,... | collective-permute-start | bytes 1179656 | tf_op jit(solution)/shard_map/ppermute | solution.py:199
  20.4 12.1 %collective-permute-start.8 = (bf16[96,2048]{1,0:T(8,128)(2,1)S(1)}, bf16[96,2048]{1,0:T(8,128)(2,1)S(1)}, u32[]{:S(2)}, u32[]{:S(2)}) collective-permute-start(bf16[96,2048]{1,0:T(8,128)(2,1)S(1)} %get-tuple-element.55), channel_id=1, source_target_pairs={{0,6},{1,7},{2,0},{3,1},{4,2},{5,3},{6,4},{7,5},{8,14},{9,15},{10,... | collective-permute-start | bytes 1179656 | tf_op jit(solution)/shard_map/ppermute | solution.py:203
  34.3 7.6 %collective-permute-start.10 = (bf16[320,2048]{1,0:T(8,128)(2,1)S(1)}, bf16[320,2048]{1,0:T(8,128)(2,1)S(1)}, u32[]{:S(2)}, u32[]{:S(2)}) collective-permute-start(bf16[320,2048]{1,0:T(8,128)(2,1)S(1)} %pack.9.refs_0_.refs_4_), channel_id=1, source_target_pairs={{0,1},{1,0},{2,3},{3,2},{4,5},{5,4},{6,7},{7,6},{8,9},{9,8},{10,11... | collective-permute-start | bytes 3932168 | tf_op jit(solution)/shard_map/ppermute | solution.py:207
  35.5 10.0 %collective-permute-start.11 = (bf16[64,2048]{1,0:T(8,128)(2,1)S(1)}, bf16[64,2048]{1,0:T(8,128)(2,1)S(1)}, u32[]{:S(2)}, u32[]{:S(2)}) collective-permute-start(bf16[64,2048]{1,0:T(8,128)(2,1)S(1)} %get-tuple-element.57), channel_id=1, source_target_pairs={{0,2},{1,3},{2,4},{3,5},{4,6},{5,7},{6,0},{7,1},{8,10},{9,11},{10,... | collective-permute-start | bytes 786440 | tf_op jit(solution)/shard_map/ppermute | solution.py:199
  35.6 9.9 %collective-permute-start.12 = (bf16[64,2048]{1,0:T(8,128)(2,1)S(1)}, bf16[64,2048]{1,0:T(8,128)(2,1)S(1)}, u32[]{:S(2)}, u32[]{:S(2)}) collective-permute-start(bf16[64,2048]{1,0:T(8,128)(2,1)S(1)} %get-tuple-element.58), channel_id=1, source_target_pairs={{0,8},{1,9},{2,10},{3,11},{4,12},{5,13},{6,14},{7,15},{8,0},{9,1},... | collective-permute-start | bytes 786440 | tf_op jit(solution)/shard_map/ppermute | solution.py:195
  36.4 9.2 %collective-permute-start.14 = (bf16[64,2048]{1,0:T(8,128)(2,1)S(1)}, bf16[64,2048]{1,0:T(8,128)(2,1)S(1)}, u32[]{:S(2)}, u32[]{:S(2)}) collective-permute-start(bf16[64,2048]{1,0:T(8,128)(2,1)S(1)} %get-tuple-element.63), channel_id=1, source_target_pairs={{0,6},{1,7},{2,0},{3,1},{4,2},{5,3},{6,4},{7,5},{8,14},{9,15},{10,... | collective-permute-start | bytes 786440 | tf_op jit(solution)/shard_map/ppermute | solution.py:203
  45.5 27.5 %copy-start.4 = (f32[512]{0:T(512)S(1)}, f32[512]{0:T(512)}, u32[]{:S(2)}) copy-start(f32[512]{0:T(512)} %param.13) | copy-start | bytes 6148
  45.5 2.4 %collective-permute-start.13 = (bf16[128,2048]{1,0:T(8,128)(2,1)S(1)}, bf16[128,2048]{1,0:T(8,128)(2,1)S(1)}, u32[]{:S(2)}, u32[]{:S(2)}) collective-permute-start(bf16[128,2048]{1,0:T(8,128)(2,1)S(1)} %pack.11.refs_2_.refs_6_), channel_id=1, source_target_pairs={{0,1},{1,0},{2,3},{3,2},{4,5},{5,4},{6,7},{7,6},{8,9},{9,8},{10,11... | collective-permute-start | bytes 1572872 | tf_op jit(solution)/shard_map/ppermute | solution.py:207
  45.6 2.3 %collective-permute-start.15 = (bf16[64,2048]{1,0:T(8,128)(2,1)S(1)}, bf16[64,2048]{1,0:T(8,128)(2,1)S(1)}, u32[]{:S(2)}, u32[]{:S(2)}) collective-permute-start(bf16[64,2048]{1,0:T(8,128)(2,1)S(1)} %collective-permute-done.14.refs_4_.refs_8_), channel_id=1, source_target_pairs={{0,1},{1,0},{2,3},{3,2},{4,5},{5,4},{6,7},{7,6},{8,9},{9,8},{10,11... | collective-permute-start | bytes 786440 | tf_op jit(solution)/shard_map/ppermute | solution.py:207
